TPU v7x, 32 devices: a whole 2x2x4 slice. The times are simulated.
32 devices in a mesh: groups: 2 (over x), expert: 16 (over z, y, core).
Axes of the slice: x: 2, y: 2, z: 4, core: 2. Of those that a mesh axis runs over, the one named last changes fastest.
Arguments:
- resid: bfloat16 [4096, 4096], P(('groups', 'expert')), parts along dimension 0, may hold values from -6 to 6
- queries: bfloat16 [4096, 4096], P(('groups', 'expert')), parts along dimension 0, may hold values from -8 to 8
- keys: bfloat16 [4096, 256], P(('groups', 'expert')), parts along dimension 0, may hold values from -6 to 6
- values: bfloat16 [4096, 256], P(('groups', 'expert')), parts along dimension 0, may hold values from -6 to 6
- doc_ids: int32 [4096], P(('groups', 'expert')), parts along dimension 0, may hold values from 0 to 3, never falling along the last dimension, each value on 1 to 1280 neighbouring positions
- norm_gain: float32 [4096], replicated, may hold values from 0.1 to 1.9
- routes: int32 [4096, 4], P(('groups', 'expert')), parts along dimension 0, may hold values from 0 to 127, as said below
- route_weights: float32 [4096, 4], P(('groups', 'expert')), parts along dimension 0, may hold values from 0.2 to 1
- w_gate: bfloat16 [16, 4096, 384], P('expert'), may hold values from -0.09375 to 0.09375
- w_up: bfloat16 [16, 4096, 384], P('expert'), may hold values from -0.09375 to 0.09375
- w_down: bfloat16 [16, 384, 4096], P('expert'), may hold values from -0.15625 to 0.15625
Outputs:
- layer_out: bfloat16 [4096, 4096], P(('groups', 'expert')), parts along dimension 0
There are 2 independent parts, one for each index of `groups`. A program takes and returns all parts, laid end to end along the dimension named above; an argument that names none is the same for every part. Nothing has to cross between parts.
Inputs may be any that keep to these rules, and one draw needn't show every extreme that they name: Each token names 4 different experts; in the tokens of one device no expert is named by more than 6 routes, and in every draw some expert below 4 is named by exactly 6 routes in the tokens of every device. `doc_ids`: document ids never fall along the sequence; no document is longer than 1280 tokens.
All inputs are finite; a program needn't handle non-finite values.
Results may differ from a plain program's by a relative error of at most 0.0045.
Values may be sent and summed in bfloat16 or wider, within the bound.
No kernel may reach another device: no remote copies, remote signals or barrier semaphores. Data moves between devices by JAX's collectives and lax.ppermute only.
A program may use at most 128 MiB of HBM per device.

v0:
```python
import functools
import math

import jax
import jax.numpy as jnp
from jax import lax
from jax.experimental import pallas as pl
from jax.experimental.pallas import tpu as pltpu
from jax.sharding import PartitionSpec as P

HEAD = 128
QUERY_HEADS = 32
KV_HEADS = 2
GROUP = QUERY_HEADS // KV_HEADS
SHARDS = 4
SLOTS = 8
TILE = 128
KEYS = 256
MSG = 256
PLANES = 4
LANES = PLANES * GROUP * SLOTS
SCALE = math.log2(math.e) / math.sqrt(HEAD)
LOW = -1e30
F32 = jnp.float32
BF16 = jnp.bfloat16
VMEM = pl.BlockSpec(memory_space=pltpu.VMEM)
SMEM = pl.BlockSpec(memory_space=pltpu.SMEM)
ANY = pl.BlockSpec(memory_space=pl.ANY)


def dot(a, b, ca=1, cb=0):
    return lax.dot_general(a, b, (((ca,), (cb,)), ((), ())), preferred_element_type=F32)


def slot_rows(routes, experts):
    members = jnp.concatenate(
        [
            jnp.max((routes == e).astype(F32), axis=0, keepdims=True)
            for e in experts
        ],
        axis=0,
    )
    count = len(experts)
    padded = -(-count // 8) * 8
    wide = members
    if padded > count:
        wide = jnp.concatenate([members, jnp.zeros((padded - count, TILE), F32)], axis=0)
    before = lax.broadcasted_iota(jnp.int32, (TILE, TILE), 0) < lax.broadcasted_iota(
        jnp.int32, (TILE, TILE), 1
    )
    ranks = dot(wide.astype(BF16), before.astype(F32).astype(BF16))
    return members, ranks


def pack_kernel(planes, pos_ref, routes_ref, docs_ref, keys_ref, values_ref, q_ref, x_ref, *outs):
    z = pos_ref[0] // SHARDS
    routes = routes_ref[...]
    experts = [lax.rem(z + k, planes) for k in range(planes)]
    members, ranks = slot_rows(routes, experts)
    docs = docs_ref[...].astype(F32)
    lane_slot = (lax.broadcasted_iota(jnp.int32, (TILE, TILE), 0) % SLOTS).astype(F32)
    token = lax.broadcasted_iota(jnp.int32, (1, TILE), 1).astype(F32)
    facts = jnp.concatenate(
        [token, docs, jnp.ones((1, TILE), F32), jnp.zeros((5, TILE), F32)], axis=0
    ).astype(BF16)
    picks = [
        jnp.where(ranks[k : k + 1] == lane_slot, members[k : k + 1], 0.0) for k in range(planes)
    ]
    chooser = jnp.concatenate([p[:SLOTS] for p in picks], axis=0).astype(BF16)
    q_rows = dot(chooser, q_ref[...])
    x_rows = dot(chooser, x_ref[...])
    value_t = jnp.concatenate(
        [
            values_ref[:, h * HEAD : (h + 1) * HEAD].astype(F32).T.astype(BF16)
            for h in range(KV_HEADS)
        ],
        axis=1,
    )
    keys = keys_ref[...]
    row = lax.broadcasted_iota(jnp.int32, (SLOTS, TILE), 0)
    for k in range(planes):
        out = outs[k]
        out[0:TILE, 0:256] = keys
        out[0:TILE, 256:512] = value_t
        known = dot(facts, picks[k].astype(BF16), 1, 1)
        place = known[0:1]
        doc = known[1:2] + (1.0 - known[2:3]) * docs[:, 0:1]
        for half, rows in ((TILE, q_rows), (TILE + 64, x_rows)):
            for pair in range(QUERY_HEADS // 2):
                two = []
                for a in (2 * pair, 2 * pair + 1):
                    block = rows[k * SLOTS : (k + 1) * SLOTS, a * HEAD : (a + 1) * HEAD]
                    if half == TILE and a == 0:
                        block = jnp.where(row == 6, docs, jnp.where(row == 7, place, block))
                    if half == TILE and a == 2:
                        block = jnp.where(row == 6, doc, block)
                    two.append(block)
                at = half + 16 * (pair // 4)
                lane = (pair % 4) * HEAD
                out[at : at + 16, lane : lane + HEAD] = jnp.concatenate(two, axis=0).astype(BF16)


def load_pieces(planes, pos, pieces, held, sems, rows):
    z, y, c = pos // SHARDS, (pos // 2) % 2, pos % 2
    copies = []
    for flip_c in range(2):
        for flip_y in range(2):
            for k in range(planes):
                at = len(copies)
                sender = (
                    lax.rem(z - k + planes, planes) * SHARDS + (y ^ flip_y) * 2 + (c ^ flip_c)
                )
                copy = pltpu.make_async_copy(
                    pieces[at].at[pl.ds(0, rows)], held.at[sender, pl.ds(0, rows)], sems.at[at]
                )
                copy.start()
                copies.append(copy)
    return copies


def doc_starts(n, held):
    sums = [jnp.zeros((1, TILE), F32) for _ in range(3)]
    for s in range(n):
        docs = held[s, TILE : TILE + 16, 0:HEAD].astype(F32)[6:7]
        for d in range(3):
            sums[d] = sums[d] + jnp.where(docs < d + 1.0, 1.0, 0.0)
    return [jnp.sum(s, axis=1, keepdims=True) for s in sums]


def starts_of(docs, starts):
    first = jnp.zeros_like(docs)
    for d in range(3):
        first = jnp.where(docs == d + 1.0, starts[d], first)
    return first


def flash(held, q_refs, kv_heads, acc_ref, place, first, low, high):
    lanes = place.shape[1]
    chains = len(q_refs)
    for i in range(chains):
        acc_ref[i] = jnp.zeros((HEAD, lanes), F32)

    def step(kb, carried):
        key_at = (
            kb * KEYS + lax.broadcasted_iota(jnp.int32, (KEYS, 1), 0)
        ).astype(F32)
        allowed = (key_at >= first) & (key_at <= place)
        out = []
        for i in range(chains):
            top, total = carried[2 * i], carried[2 * i + 1]
            h = kv_heads[i]
            keys = jnp.concatenate(
                [held[2 * kb + t, 0:TILE, h * HEAD : (h + 1) * HEAD] for t in range(2)], axis=0
            )
            values = jnp.concatenate(
                [held[2 * kb + t, 0:TILE, 256 + h * HEAD : 384 + h * HEAD] for t in range(2)],
                axis=1,
            )
            scores = jnp.where(allowed, dot(keys, q_refs[i][...], 1, 1), LOW)
            new_top = jnp.maximum(top, jnp.max(scores, axis=0, keepdims=True))
            factor = jnp.exp2((top - new_top) * SCALE)
            weights = jnp.exp2((scores - new_top) * SCALE)
            acc_ref[i] = acc_ref[i] * factor + dot(values, weights.astype(BF16))
            out += [new_top, total * factor + jnp.sum(weights, axis=0, keepdims=True)]
        return tuple(out)

    init = (jnp.full((1, lanes), LOW, F32), jnp.zeros((1, lanes), F32)) * chains
    final = lax.fori_loop(low, high, step, init)
    return [(acc_ref[i] / final[2 * i + 1]).T for i in range(chains)]


def expert_kernel(n, pos_ref, gain_ref, *refs):
    planes = n // SHARDS
    pieces = refs[:n]
    weights = refs[n : n + 3]
    keep_ref, send_ref = refs[n + 3 : n + 5]
    held, q_scr, acc, state, wg, wu, wd, sems = refs[n + 5 :]
    pos = pos_ref[0]
    z, y, c = pos // SHARDS, (pos // 2) % 2, pos % 2
    copies = load_pieces(planes, pos, pieces, held, sems, MSG)
    loads = []
    for i, (src, dst) in enumerate(zip(weights, (wg, wu, wd))):
        load = pltpu.make_async_copy(src.at[0], dst, sems.at[n + i])
        load.start()
        loads.append(load)
    for copy in copies:
        copy.wait()
    starts = doc_starts(n, held)
    groups = planes // PLANES

    def attend(group, kk):
        plane = lax.rem(z + group * PLANES + kk, planes)
        senders = [
            plane * SHARDS + (y ^ flip_y) * 2 + (c ^ flip_c)
            for flip_c in range(2)
            for flip_y in range(2)
        ]
        place, docs = [], []
        for i, s in enumerate(senders):
            place.append(
                held[s, TILE : TILE + 16, 0:HEAD].astype(F32)[7:8]
                + (s * TILE).astype(F32)
            )
            docs.append(held[s, TILE : TILE + 16, HEAD : 2 * HEAD].astype(F32)[6:7])
            for a in range(QUERY_HEADS // 2):
                at = TILE + 16 * (a // 4)
                lane = (a % 4) * HEAD
                q_scr[a // 8, i * TILE + (a % 8) * 16 : i * TILE + (a % 8) * 16 + 16, :] = held[
                    s, at : at + 16, lane : lane + HEAD
                ]
        place = jnp.concatenate(place, axis=1)
        first = starts_of(jnp.concatenate(docs, axis=1), starts)
        low = jnp.min(first).astype(jnp.int32) // KEYS
        high = (plane + 1) * (SHARDS * TILE // KEYS)
        done = flash(held, [q_scr.at[0], q_scr.at[1]], [0, 1], acc, place, first, low, high)
        row = pl.multiple_of(kk * SLOTS, SLOTS)
        for i, s in enumerate(senders):
            for a in range(QUERY_HEADS // 2):
                at = TILE + 64 + 16 * (a // 4)
                lane = (a % 4) * HEAD
                resid = held[s, at : at + 16, lane : lane + HEAD].astype(F32)
                rows = done[a // 8][i * TILE + (a % 8) * 16 : i * TILE + (a % 8) * 16 + 16]
                total = resid + rows
                state[pl.ds(i * PLANES * SLOTS + row, SLOTS), 2 * a * HEAD : (2 * a + 1) * HEAD] = (
                    total[0:SLOTS]
                )
                state[
                    pl.ds(i * PLANES * SLOTS + row, SLOTS),
                    (2 * a + 1) * HEAD : (2 * a + 2) * HEAD,
                ] = total[SLOTS:]

    def group_step(group):
        lax.fori_loop(0, PLANES, lambda kk, _: (attend(group, kk), 0)[1], 0)
        hidden = state[...]
        mean = jnp.mean(hidden * hidden, axis=1, keepdims=True)
        normed = (hidden * lax.rsqrt(mean + 1e-06) * gain_ref[...]).astype(BF16)
        if groups == 1:
            for load in loads:
                load.wait()
        gate = dot(normed, wg[...])
        up = dot(normed, wu[...])
        act = (gate / (1.0 + jnp.exp(-gate)) * up).astype(BF16)
        width = 1024
        for col in range(0, hidden.shape[1], width):
            part = dot(act, wd[:, col : col + width]).astype(BF16)
            half = 2 * PLANES * SLOTS
            keep_ref[group, :, col : col + width] = part[:half]
            send_ref[group, :, col : col + width] = part[half:]

    if groups == 1:
        group_step(0)
    else:
        for load in loads:
            load.wait()
        lax.fori_loop(0, groups, lambda g, _: (group_step(g), 0)[1], 0)


def own_kernel(n, kv_head, pos_ref, q_ref, x_ref, _, *refs):
    pieces = refs[:n]
    h_ref = refs[n]
    held, q_scr, acc, sems = refs[n + 1 :]
    pos = pos_ref[0]
    copies = load_pieces(n // SHARDS, pos, pieces, held, sems, TILE + 16)
    for a in range(GROUP):
        q_scr[a // 4, (a % 4) * TILE : (a % 4 + 1) * TILE, :] = q_ref[:, a * HEAD : (a + 1) * HEAD]
    for copy in copies:
        copy.wait()
    starts = doc_starts(n, held)
    docs = held[pos, TILE : TILE + 16, 0:HEAD].astype(F32)[6:7]
    first = starts_of(docs, starts)
    low = jnp.min(first).astype(jnp.int32) // KEYS
    high = pos // (KEYS // TILE) + 1
    place = (pos * TILE + lax.broadcasted_iota(jnp.int32, (1, TILE), 1)).astype(F32)
    place = jnp.concatenate([place] * 4, axis=1)
    first = jnp.concatenate([first] * 4, axis=1)
    for pair in range(2):
        done = flash(
            held,
            [q_scr.at[2 * pair], q_scr.at[2 * pair + 1]],
            [kv_head, kv_head],
            acc,
            place,
            first,
            low,
            high,
        )
        for i in range(2):
            for g in range(4):
                lane = (pair * 8 + i * 4 + g) * HEAD
                h_ref[:, lane : lane + HEAD] = (
                    x_ref[:, lane : lane + HEAD].astype(F32) + done[i][g * TILE : (g + 1) * TILE]
                )


def combine_kernel(planes, pos_ref, routes_ref, gates_ref, h0_ref, h1_ref, *refs):
    parts, out_ref = refs[:planes], refs[planes]
    z = pos_ref[0] // SHARDS
    routes = routes_ref[...]
    gates = gates_ref[...]
    experts = [lax.rem(z - k + planes, planes) for k in range(planes)]
    members, ranks = slot_rows(routes, experts)
    slot = lax.broadcasted_iota(jnp.int32, (SLOTS, TILE), 0).astype(F32)
    mix = []
    for k, e in enumerate(experts):
        gate = jnp.sum(jnp.where(routes == e, gates, 0.0), axis=0, keepdims=True)
        mix.append(jnp.where(ranks[k : k + 1] == slot, gate, 0.0))
    mix = jnp.concatenate(mix, axis=0).T
    mix_high = mix.astype(BF16)
    mix_low = (mix - mix_high.astype(F32)).astype(BF16)
    rows = jnp.concatenate([p[...].astype(F32) for p in parts], axis=0).astype(BF16)
    half = h0_ref.shape[1]
    for i, h in enumerate((h0_ref, h1_ref)):
        part = rows[:, i * half : (i + 1) * half]
        out_ref[:, i * half : (i + 1) * half] = (
            h[...] + dot(mix_high, part) + dot(mix_low, part)
        ).astype(BF16)


def params(mib):
    return pltpu.CompilerParams(vmem_limit_bytes=mib * 1024 * 1024)


def local(
    resid, queries, keys, values, doc_ids, norm_gain, routes, route_weights, w_gate, w_up, w_down
):
    n = lax.axis_size("expert")
    planes = n // SHARDS
    index = lax.axis_index("expert")
    pos = index.astype(jnp.int32).reshape(1)
    tokens, width = queries.shape
    hidden = w_gate.shape[2]
    routes_t = routes.T
    gates_t = route_weights.T
    message = jax.ShapeDtypeStruct((MSG, 512), BF16)

    messages = pl.pallas_call(
        functools.partial(pack_kernel, planes),
        out_shape=[message] * planes,
        in_specs=[SMEM] + [VMEM] * 6,
        out_specs=[VMEM] * planes,
        compiler_params=params(40),
        name="pack",
    )(pos, routes_t, doc_ids.reshape(1, tokens), keys, values, queries, resid)

    def move(value, target):
        return lax.ppermute(value, "expert", [(s, target(s)) for s in range(n)])

    pieces = [messages[0]]
    for k in range(1, planes):
        pieces.append(move(messages[k], lambda s: (s + k * SHARDS) % n))
    pieces = pieces + [move(p, lambda s: s ^ 2) for p in pieces]
    pieces = pieces + [move(p, lambda s: s ^ 1) for p in pieces]

    groups = planes // PLANES
    half = jax.ShapeDtypeStruct((groups, 2 * PLANES * SLOTS, width), BF16)
    keep, send = pl.pallas_call(
        functools.partial(expert_kernel, n),
        out_shape=[half, half],
        in_specs=[SMEM, VMEM] + [ANY] * (n + 3),
        out_specs=[VMEM, VMEM],
        scratch_shapes=[
            pltpu.VMEM((n, MSG, 512), BF16),
            pltpu.VMEM((KV_HEADS, LANES, HEAD), BF16),
            pltpu.VMEM((KV_HEADS, HEAD, LANES), F32),
            pltpu.VMEM((4 * PLANES * SLOTS, width), F32),
            pltpu.VMEM((width, hidden), BF16),
            pltpu.VMEM((width, hidden), BF16),
            pltpu.VMEM((hidden, width), BF16),
            pltpu.SemaphoreType.DMA((n + 3,)),
        ],
        compiler_params=params(40 if n <= 16 else 60),
        cost_estimate=pl.CostEstimate(
            flops=4_000_000_000, bytes_accessed=16_000_000, transcendentals=4_000_000
        ),
        name="expert",
    )(pos, norm_gain.reshape(1, width), *pieces, w_gate, w_up, w_down)

    halves = []
    for h in range(KV_HEADS):
        columns = slice(h * width // 2, (h + 1) * width // 2)
        halves.append(
            pl.pallas_call(
                functools.partial(own_kernel, n, h),
                out_shape=jax.ShapeDtypeStruct((tokens, width // 2), F32),
                in_specs=[
                    SMEM,
                    pl.BlockSpec((tokens, width // 2), lambda i, h=h: (0, h)),
                    pl.BlockSpec((tokens, width // 2), lambda i, h=h: (0, h)),
                    ANY,
                ]
                + [ANY] * n,
                out_specs=pl.BlockSpec((tokens, width // 2), lambda i: (0, 0)),
                grid=(1,),
                scratch_shapes=[
                    pltpu.VMEM((n, TILE + 16, 512), BF16),
                    pltpu.VMEM((4, 4 * TILE, HEAD), BF16),
                    pltpu.VMEM((2, HEAD, 4 * TILE), F32),
                    pltpu.SemaphoreType.DMA((n,)),
                ],
                compiler_params=params(40),
                cost_estimate=pl.CostEstimate(
                    flops=4_000_000_000, bytes_accessed=8_000_000, transcendentals=4_000_000
                ),
                name="own",
            )(pos, queries, resid, keep, *pieces)
        )

    total = keep.astype(F32) + move(send, lambda s: s ^ 1).astype(F32)
    quarter = PLANES * SLOTS
    other = move(total[:, quarter:].astype(BF16), lambda s: s ^ 2)
    total = (total[:, :quarter] + other.astype(F32)).astype(BF16)
    total = total.reshape(planes, SLOTS, width)
    parts = [total[0]]
    for k in range(1, planes):
        parts.append(move(total[k], lambda s: (s + k * SHARDS) % n))

    return pl.pallas_call(
        functools.partial(combine_kernel, planes),
        out_shape=jax.ShapeDtypeStruct((tokens, width), BF16),
        in_specs=[SMEM] + [VMEM] * (4 + planes),
        out_specs=VMEM,
        compiler_params=params(40),
        name="combine",
    )(pos, routes_t, gates_t, *halves, *parts)


def solution(mesh):
    rows = P(("groups", "expert"), None)
    in_specs = (rows,) * 4 + (P(("groups", "expert")), P(), rows, rows) + (
        P("expert", None, None),
    ) * 3
    return jax.shard_map(local, mesh=mesh, in_specs=in_specs, out_specs=rows, check_vma=False)
```

profile of v0, /device:TPU:26, one launch (start us, length us, event | category | flops | bytes accessed | tf_op | source)
XLA Modules:
  0.0 113.9 jit_solution(3674919398497319939)
XLA Ops:
  0.0 1.2 %copy-done = bf16[128,4096]{1,0:T(8,128)(2,1)S(1)} copy-done((bf16[128,4096]{1,0:T(8,128)(2,1)S(1)}, bf16[128,4096]{1,0:T(8,128)(2,1)}, u32[]{:S(2)}) %copy-start) | copy-done | bytes 1048600
  1.2 1.2 %copy-done.2 = bf16[128,4096]{1,0:T(8,128)(2,1)S(1)} copy-done((bf16[128,4096]{1,0:T(8,128)(2,1)S(1)}, bf16[128,4096]{1,0:T(8,128)(2,1)}, u32[]{:S(2)}) %copy-start.2) | copy-done | bytes 1048600
  2.5 0.8 copy-done.4
  3.3 0.8 copy-done.5
  4.1 0.7 copy-done.6
  4.8 0.7 copy-done.9
  5.5 0.6 pack.1
  6.1 0.3 collective-permute-start
  6.3 1.7 %collective-permute-start.1 = (bf16[256,512]{1,0:T(8,128)(2,1)S(1)}, bf16[256,512]{1,0:T(8,128)(2,1)S(1)}, u32[]{:S(2)}, u32[]{:S(2)}) collective-permute-start(bf16[256,512]{1,0:T(8,128)(2,1)S(1)} %get-tuple-element.13), channel_id=1, source_target_pairs={{0,8},{1,9},{2,10},{3,11},{4,12},{5,13},{6,14},{7,15},{8,0},{9,1},... | collective-permute-start | bytes 786440 | tf_op jit(solution)/shard_map/ppermute | solution.py:346
  8.0 0.5 collective-permute-start.2
  8.5 1.5 %collective-permute-start.3 = (bf16[256,512]{1,0:T(8,128)(2,1)S(1)}, bf16[256,512]{1,0:T(8,128)(2,1)S(1)}, u32[]{:S(2)}, u32[]{:S(2)}) collective-permute-start(bf16[256,512]{1,0:T(8,128)(2,1)S(1)} %get-tuple-element.11.refs_0_), channel_id=1, source_target_pairs={{0,2},{1,3},{2,0},{3,1},{4,6},{5,7},{6,4},{7,5},{8,10},{9,11},{10,... | collective-permute-start | bytes 786440 | tf_op jit(solution)/shard_map/ppermute | solution.py:346
  10.0 4.5 %collective-permute-done.refs_1_ = bf16[256,512]{1,0:T(8,128)(2,1)S(1)} collective-permute-done((bf16[256,512]{1,0:T(8,128)(2,1)S(1)}, bf16[256,512]{1,0:T(8,128)(2,1)S(1)}, u32[]{:S(2)}, u32[]{:S(2)}) %collective-permute-start) | collective-permute-done | bytes 262176 | tf_op jit(solution)/shard_map/ppermute | solution.py:346
  14.6 0.0 collective-permute-start.8
  14.6 16.4 %collective-permute-done.1.refs_2_ = bf16[256,512]{1,0:T(8,128)(2,1)S(1)} collective-permute-done((bf16[256,512]{1,0:T(8,128)(2,1)S(1)}, bf16[256,512]{1,0:T(8,128)(2,1)S(1)}, u32[]{:S(2)}, u32[]{:S(2)}) %collective-permute-start.1) | collective-permute-done | bytes 262176 | tf_op jit(solution)/shard_map/ppermute | solution.py:346
  30.9 1.5 %collective-permute-start.4 = (bf16[256,512]{1,0:T(8,128)(2,1)S(1)}, bf16[256,512]{1,0:T(8,128)(2,1)S(1)}, u32[]{:S(2)}, u32[]{:S(2)}) collective-permute-start(bf16[256,512]{1,0:T(8,128)(2,1)S(1)} %collective-permute-done.refs_1_), channel_id=1, source_target_pairs={{0,2},{1,3},{2,0},{3,1},{4,6},{5,7},{6,4},{7,5},{8,10},{9,11},{10,... | collective-permute-start | bytes 786440 | tf_op jit(solution)/shard_map/ppermute | solution.py:346
  32.4 0.0 collective-permute-done.7.refs_8_
  32.4 0.6 collective-permute-start.5
  33.0 0.0 collective-permute-done.3.refs_4_
  33.0 1.5 %collective-permute-start.6 = (bf16[256,512]{1,0:T(8,128)(2,1)S(1)}, bf16[256,512]{1,0:T(8,128)(2,1)S(1)}, u32[]{:S(2)}, u32[]{:S(2)}) collective-permute-start(bf16[256,512]{1,0:T(8,128)(2,1)S(1)} %collective-permute-done.2.refs_3_), channel_id=1, source_target_pairs={{0,2},{1,3},{2,0},{3,1},{4,6},{5,7},{6,4},{7,5},{8,10},{9,11},{10,... | collective-permute-start | bytes 786440 | tf_op jit(solution)/shard_map/ppermute | solution.py:346
  34.5 0.0 collective-permute-done.8.refs_9_
  34.5 0.0 collective-permute-start.10
  34.5 5.6 %collective-permute-done.4.refs_5_ = bf16[256,512]{1,0:T(8,128)(2,1)S(1)} collective-permute-done((bf16[256,512]{1,0:T(8,128)(2,1)S(1)}, bf16[256,512]{1,0:T(8,128)(2,1)S(1)}, u32[]{:S(2)}, u32[]{:S(2)}) %collective-permute-start.4) | collective-permute-done | bytes 262176 | tf_op jit(solution)/shard_map/ppermute | solution.py:346
  40.2 0.0 collective-permute-done.9.refs_10_
  40.2 0.5 collective-permute-start.12
  40.7 5.1 %collective-permute-done.5.refs_6_ = bf16[256,512]{1,0:T(8,128)(2,1)S(1)} collective-permute-done((bf16[256,512]{1,0:T(8,128)(2,1)S(1)}, bf16[256,512]{1,0:T(8,128)(2,1)S(1)}, u32[]{:S(2)}, u32[]{:S(2)}) %collective-permute-start.5) | collective-permute-done | bytes 262176 | tf_op jit(solution)/shard_map/ppermute | solution.py:346
  45.8 0.0 collective-permute-start.13
  45.8 3.5 %collective-permute-done.6.refs_7_ = bf16[256,512]{1,0:T(8,128)(2,1)S(1)} collective-permute-done((bf16[256,512]{1,0:T(8,128)(2,1)S(1)}, bf16[256,512]{1,0:T(8,128)(2,1)S(1)}, u32[]{:S(2)}, u32[]{:S(2)}) %collective-permute-start.6) | collective-permute-done | bytes 262176 | tf_op jit(solution)/shard_map/ppermute | solution.py:346
  49.3 0.0 collective-permute-done.11.refs_12_
  49.3 0.0 collective-permute-done.12.refs_13_
  49.4 1.5 %collective-permute-done.14.refs_15_ = bf16[256,512]{1,0:T(8,128)(2,1)S(1)} collective-permute-done((bf16[256,512]{1,0:T(8,128)(2,1)S(1)}, bf16[256,512]{1,0:T(8,128)(2,1)S(1)}, u32[]{:S(2)}, u32[]{:S(2)}) %collective-permute-start.14) | collective-permute-done | bytes 262176 | tf_op jit(solution)/shard_map/ppermute | solution.py:346
  50.9 1.9 %copy-done.10 = bf16[1,4096,384]{2,1,0:T(8,128)(2,1)S(1)} copy-done((bf16[1,4096,384]{2,1,0:T(8,128)(2,1)S(1)}, bf16[1,4096,384]{2,1,0:T(8,128)(2,1)}, u32[]{:S(2)}) %copy-start.10) | copy-done | bytes 3145752
  52.8 1.9 %copy-done.11 = bf16[1,4096,384]{2,1,0:T(8,128)(2,1)S(1)} copy-done((bf16[1,4096,384]{2,1,0:T(8,128)(2,1)S(1)}, bf16[1,4096,384]{2,1,0:T(8,128)(2,1)}, u32[]{:S(2)}) %copy-start.11) | copy-done | bytes 3145752
  54.6 0.7 copy-done.12
  55.4 20.0 %expert.1 = (bf16[1,64,4096]{2,1,0:T(8,128)(2,1)S(1)}, bf16[1,64,4096]{2,1,0:T(8,128)(2,1)S(1)}) custom-call(s32[1]{0:T(128)} %bitcast.pos_ref, f32[1,4096]{1,0:T(1,128)S(1)} %bitcast.17, bf16[256,512]{1,0:T(8,128)(2,1)S(1)} %get-tuple-element.11.refs_0_, bf16[256,512]{1,0:T(8,128)(2,1)S(1)} %collective-permute-done.refs_1_, ...), custom_call_target="tpu_custom_call" | custom-call | flops 4000000000 | bytes 16000000 | tf_op jit(solution)/shard_map/expert/pallas_call | solution.py:356
  75.4 0.2 collective-permute-start.15
  75.5 1.8 %collective-permute-done.15 = bf16[1,64,4096]{2,1,0:T(8,128)(2,1)S(1)} collective-permute-done((bf16[1,64,4096]{2,1,0:T(8,128)(2,1)S(1)}, bf16[1,64,4096]{2,1,0:T(8,128)(2,1)S(1)}, u32[]{:S(2)}, u32[]{:S(2)}) %collective-permute-start.15) | collective-permute-done | bytes 524320 | tf_op jit(solution)/shard_map/ppermute | solution.py:346
  77.3 0.1 convert_add_fusion
  77.5 1.6 %collective-permute-start.16 = (bf16[1,32,4096]{2,1,0:T(8,128)(2,1)S(1)}, bf16[1,32,4096]{2,1,0:T(8,128)(2,1)S(1)}, u32[]{:S(2)}, u32[]{:S(2)}) collective-permute-start(bf16[1,32,4096]{2,1,0:T(8,128)(2,1)S(1)} %slice.43), channel_id=1, source_target_pairs={{0,2},{1,3},{2,0},{3,1},{4,6},{5,7},{6,4},{7,5},{8,10},{9,11},{10,... | collective-permute-start | bytes 786440 | tf_op jit(solution)/shard_map/ppermute | solution.py:346
  79.1 14.4 %own.3.h1_ref = f32[128,2048]{1,0:T(8,128)S(1)} custom-call(s32[1]{0:T(128)} %bitcast.pos_ref, bf16[128,4096]{1,0:T(8,128)(2,1)S(1)} %copy-done.1, bf16[128,4096]{1,0:T(8,128)(2,1)S(1)} %copy-done.3, bf16[1,64,4096]{2,1,0:T(8,128)(2,1)S(1)} %get-tuple-element.15._, bf16[256,512]{1,0:T(8,128)(2,1)S(1)} %get-tuple-element.11.refs_0_, ...), custom_call_target="tpu_custom_call" | custom-call | flops 4000000000 | bytes 8000000 | tf_op jit(solution)/shard_map/own/pallas_call | solution.py:382
  93.5 0.0 collective-permute-done.16
  93.6 0.1 collective-permute-start.19
  93.7 0.1 collective-permute-start.18
  93.7 0.0 copy-start.7
  93.8 0.0 copy-start.8
  93.8 3.7 %collective-permute-start.17 = (bf16[8,4096]{1,0:T(8,128)(2,1)S(1)}, bf16[8,4096]{1,0:T(8,128)(2,1)S(1)}, u32[]{:S(2)}, u32[]{:S(2)}) collective-permute-start(bf16[8,4096]{1,0:T(8,128)(2,1)S(1)} %get-tuple-element.19), channel_id=1, source_target_pairs={{0,4},{1,5},{2,6},{3,7},{4,8},{5,9},{6,10},{7,11},{8,12},{9,13},{1... | collective-permute-start | bytes 196616 | tf_op jit(solution)/shard_map/ppermute | solution.py:346
  97.5 14.4 %own.2.h0_ref = f32[128,2048]{1,0:T(8,128)S(1)} custom-call(s32[1]{0:T(128)} %bitcast.pos_ref, bf16[128,4096]{1,0:T(8,128)(2,1)S(1)} %copy-done.1, bf16[128,4096]{1,0:T(8,128)(2,1)S(1)} %copy-done.3, bf16[1,64,4096]{2,1,0:T(8,128)(2,1)S(1)} %get-tuple-element.15._, bf16[256,512]{1,0:T(8,128)(2,1)S(1)} %get-tuple-element.11.refs_0_, ...), custom_call_target="tpu_custom_call" | custom-call | flops 4000000000 | bytes 8000000 | tf_op jit(solution)/shard_map/own/pallas_call | solution.py:382
  111.9 0.0 collective-permute-done.19.refs_3_
  112.0 1.9 %combine.1 = bf16[128,4096]{1,0:T(8,128)(2,1)} custom-call(s32[1]{0:T(128)} %bitcast.pos_ref, s32[4,128]{1,0:T(4,128)S(1)} %bitcast.14, f32[4,128]{1,0:T(4,128)S(1)} %bitcast.15, f32[128,2048]{1,0:T(8,128)S(1)} %own.2.h0_ref, f32[128,2048]{1,0:T(8,128)S(1)} %own.3.h1_ref, bf16[8,4096]{1,0:T(8,128)(2,1)S(1)} %get-tuple-element.20.refs_0_, ...), custom_call_target="tpu_custom_call" | custom-call | tf_op jit(solution)/shard_map/combine/pallas_call | solution.py:417
  (27 shorter events, 0.1 us)
Async XLA Ops:
  0.0 1.2 %copy-start = (bf16[128,4096]{1,0:T(8,128)(2,1)S(1)}, bf16[128,4096]{1,0:T(8,128)(2,1)}, u32[]{:S(2)}) copy-start(bf16[128,4096]{1,0:T(8,128)(2,1)} %q_ref.5) | copy-start | bytes 3145732
  1.2 1.2 %copy-start.2 = (bf16[128,4096]{1,0:T(8,128)(2,1)S(1)}, bf16[128,4096]{1,0:T(8,128)(2,1)}, u32[]{:S(2)}) copy-start(bf16[128,4096]{1,0:T(8,128)(2,1)} %x_ref.5) | copy-start | bytes 3145732
  2.5 0.8 copy-start.4
  3.3 0.8 copy-start.5
  4.1 0.7 copy-start.6
  4.8 0.7 copy-start.9
  6.1 8.5 %collective-permute-start = (bf16[256,512]{1,0:T(8,128)(2,1)S(1)}, bf16[256,512]{1,0:T(8,128)(2,1)S(1)}, u32[]{:S(2)}, u32[]{:S(2)}) collective-permute-start(bf16[256,512]{1,0:T(8,128)(2,1)S(1)} %get-tuple-element.12), channel_id=1, source_target_pairs={{0,4},{1,5},{2,6},{3,7},{4,8},{5,9},{6,10},{7,11},{8,12},{9,13},{1... | collective-permute-start | bytes 786440 | tf_op jit(solution)/shard_map/ppermute | solution.py:346
  6.3 24.6 %collective-permute-start.1 = (bf16[256,512]{1,0:T(8,128)(2,1)S(1)}, bf16[256,512]{1,0:T(8,128)(2,1)S(1)}, u32[]{:S(2)}, u32[]{:S(2)}) collective-permute-start(bf16[256,512]{1,0:T(8,128)(2,1)S(1)} %get-tuple-element.13), channel_id=1, source_target_pairs={{0,8},{1,9},{2,10},{3,11},{4,12},{5,13},{6,14},{7,15},{8,0},{9,1},... | collective-permute-start | bytes 786440 | tf_op jit(solution)/shard_map/ppermute | solution.py:346
  8.0 24.4 %collective-permute-start.2 = (bf16[256,512]{1,0:T(8,128)(2,1)S(1)}, bf16[256,512]{1,0:T(8,128)(2,1)S(1)}, u32[]{:S(2)}, u32[]{:S(2)}) collective-permute-start(bf16[256,512]{1,0:T(8,128)(2,1)S(1)} %get-tuple-element.14), channel_id=1, source_target_pairs={{0,12},{1,13},{2,14},{3,15},{4,0},{5,1},{6,2},{7,3},{8,4},{9,5},{1... | collective-permute-start | bytes 786440 | tf_op jit(solution)/shard_map/ppermute | solution.py:346
  8.5 23.9 %collective-permute-start.7 = (bf16[256,512]{1,0:T(8,128)(2,1)S(1)}, bf16[256,512]{1,0:T(8,128)(2,1)S(1)}, u32[]{:S(2)}, u32[]{:S(2)}) collective-permute-start(bf16[256,512]{1,0:T(8,128)(2,1)S(1)} %get-tuple-element.11.refs_0_), channel_id=1, source_target_pairs={{0,1},{1,0},{2,3},{3,2},{4,5},{5,4},{6,7},{7,6},{8,9},{9,8},{10,11... | collective-permute-start | bytes 786440 | tf_op jit(solution)/shard_map/ppermute | solution.py:346
  8.5 24.5 %collective-permute-start.3 = (bf16[256,512]{1,0:T(8,128)(2,1)S(1)}, bf16[256,512]{1,0:T(8,128)(2,1)S(1)}, u32[]{:S(2)}, u32[]{:S(2)}) collective-permute-start(bf16[256,512]{1,0:T(8,128)(2,1)S(1)} %get-tuple-element.11.refs_0_), channel_id=1, source_target_pairs={{0,2},{1,3},{2,0},{3,1},{4,6},{5,7},{6,4},{7,5},{8,10},{9,11},{10,... | collective-permute-start | bytes 786440 | tf_op jit(solution)/shard_map/ppermute | solution.py:346
  14.6 20.0 %collective-permute-start.8 = (bf16[256,512]{1,0:T(8,128)(2,1)S(1)}, bf16[256,512]{1,0:T(8,128)(2,1)S(1)}, u32[]{:S(2)}, u32[]{:S(2)}) collective-permute-start(bf16[256,512]{1,0:T(8,128)(2,1)S(1)} %collective-permute-done.refs_1_), channel_id=1, source_target_pairs={{0,1},{1,0},{2,3},{3,2},{4,5},{5,4},{6,7},{7,6},{8,9},{9,8},{10,11... | collective-permute-start | bytes 786440 | tf_op jit(solution)/shard_map/ppermute | solution.py:346
  30.9 9.2 %collective-permute-start.4 = (bf16[256,512]{1,0:T(8,128)(2,1)S(1)}, bf16[256,512]{1,0:T(8,128)(2,1)S(1)}, u32[]{:S(2)}, u32[]{:S(2)}) collective-permute-start(bf16[256,512]{1,0:T(8,128)(2,1)S(1)} %collective-permute-done.refs_1_), channel_id=1, source_target_pairs={{0,2},{1,3},{2,0},{3,1},{4,6},{5,7},{6,4},{7,5},{8,10},{9,11},{10,... | collective-permute-start | bytes 786440 | tf_op jit(solution)/shard_map/ppermute | solution.py:346
  32.4 7.7 %collective-permute-start.9 = (bf16[256,512]{1,0:T(8,128)(2,1)S(1)}, bf16[256,512]{1,0:T(8,128)(2,1)S(1)}, u32[]{:S(2)}, u32[]{:S(2)}) collective-permute-start(bf16[256,512]{1,0:T(8,128)(2,1)S(1)} %collective-permute-done.1.refs_2_), channel_id=1, source_target_pairs={{0,1},{1,0},{2,3},{3,2},{4,5},{5,4},{6,7},{7,6},{8,9},{9,8},{10,11... | collective-permute-start | bytes 786440 | tf_op jit(solution)/shard_map/ppermute | solution.py:346
  32.4 13.3 %collective-permute-start.5 = (bf16[256,512]{1,0:T(8,128)(2,1)S(1)}, bf16[256,512]{1,0:T(8,128)(2,1)S(1)}, u32[]{:S(2)}, u32[]{:S(2)}) collective-permute-start(bf16[256,512]{1,0:T(8,128)(2,1)S(1)} %collective-permute-done.1.refs_2_), channel_id=1, source_target_pairs={{0,2},{1,3},{2,0},{3,1},{4,6},{5,7},{6,4},{7,5},{8,10},{9,11},{10,... | collective-permute-start | bytes 786440 | tf_op jit(solution)/shard_map/ppermute | solution.py:346
  33.0 16.3 %collective-permute-start.6 = (bf16[256,512]{1,0:T(8,128)(2,1)S(1)}, bf16[256,512]{1,0:T(8,128)(2,1)S(1)}, u32[]{:S(2)}, u32[]{:S(2)}) collective-permute-start(bf16[256,512]{1,0:T(8,128)(2,1)S(1)} %collective-permute-done.2.refs_3_), channel_id=1, source_target_pairs={{0,2},{1,3},{2,0},{3,1},{4,6},{5,7},{6,4},{7,5},{8,10},{9,11},{10,... | collective-permute-start | bytes 786440 | tf_op jit(solution)/shard_map/ppermute | solution.py:346
  34.5 14.8 %collective-permute-start.10 = (bf16[256,512]{1,0:T(8,128)(2,1)S(1)}, bf16[256,512]{1,0:T(8,128)(2,1)S(1)}, u32[]{:S(2)}, u32[]{:S(2)}) collective-permute-start(bf16[256,512]{1,0:T(8,128)(2,1)S(1)} %collective-permute-done.2.refs_3_), channel_id=1, source_target_pairs={{0,1},{1,0},{2,3},{3,2},{4,5},{5,4},{6,7},{7,6},{8,9},{9,8},{10,11... | collective-permute-start | bytes 786440 | tf_op jit(solution)/shard_map/ppermute | solution.py:346
  40.2 9.2 %collective-permute-start.11 = (bf16[256,512]{1,0:T(8,128)(2,1)S(1)}, bf16[256,512]{1,0:T(8,128)(2,1)S(1)}, u32[]{:S(2)}, u32[]{:S(2)}) collective-permute-start(bf16[256,512]{1,0:T(8,128)(2,1)S(1)} %collective-permute-done.3.refs_4_), channel_id=1, source_target_pairs={{0,1},{1,0},{2,3},{3,2},{4,5},{5,4},{6,7},{7,6},{8,9},{9,8},{10,11... | collective-permute-start | bytes 786440 | tf_op jit(solution)/shard_map/ppermute | solution.py:346
  40.2 9.2 %collective-permute-start.12 = (bf16[256,512]{1,0:T(8,128)(2,1)S(1)}, bf16[256,512]{1,0:T(8,128)(2,1)S(1)}, u32[]{:S(2)}, u32[]{:S(2)}) collective-permute-start(bf16[256,512]{1,0:T(8,128)(2,1)S(1)} %collective-permute-done.4.refs_5_), channel_id=1, source_target_pairs={{0,1},{1,0},{2,3},{3,2},{4,5},{5,4},{6,7},{7,6},{8,9},{9,8},{10,11... | collective-permute-start | bytes 786440 | tf_op jit(solution)/shard_map/ppermute | solution.py:346
  45.8 3.6 %collective-permute-start.13 = (bf16[256,512]{1,0:T(8,128)(2,1)S(1)}, bf16[256,512]{1,0:T(8,128)(2,1)S(1)}, u32[]{:S(2)}, u32[]{:S(2)}) collective-permute-start(bf16[256,512]{1,0:T(8,128)(2,1)S(1)} %collective-permute-done.5.refs_6_), channel_id=1, source_target_pairs={{0,1},{1,0},{2,3},{3,2},{4,5},{5,4},{6,7},{7,6},{8,9},{9,8},{10,11... | collective-permute-start | bytes 786440 | tf_op jit(solution)/shard_map/ppermute | solution.py:346
  49.3 1.5 %collective-permute-start.14 = (bf16[256,512]{1,0:T(8,128)(2,1)S(1)}, bf16[256,512]{1,0:T(8,128)(2,1)S(1)}, u32[]{:S(2)}, u32[]{:S(2)}) collective-permute-start(bf16[256,512]{1,0:T(8,128)(2,1)S(1)} %collective-permute-done.6.refs_7_), channel_id=1, source_target_pairs={{0,1},{1,0},{2,3},{3,2},{4,5},{5,4},{6,7},{7,6},{8,9},{9,8},{10,11... | collective-permute-start | bytes 786440 | tf_op jit(solution)/shard_map/ppermute | solution.py:346
  50.9 1.9 %copy-start.10 = (bf16[1,4096,384]{2,1,0:T(8,128)(2,1)S(1)}, bf16[1,4096,384]{2,1,0:T(8,128)(2,1)}, u32[]{:S(2)}) copy-start(bf16[1,4096,384]{2,1,0:T(8,128)(2,1)} %refs_16_.1) | copy-start | bytes 9437188
  52.7 1.9 %copy-start.11 = (bf16[1,4096,384]{2,1,0:T(8,128)(2,1)S(1)}, bf16[1,4096,384]{2,1,0:T(8,128)(2,1)}, u32[]{:S(2)}) copy-start(bf16[1,4096,384]{2,1,0:T(8,128)(2,1)} %refs_17_.1) | copy-start | bytes 9437188
  54.6 0.7 copy-start.12
  55.4 23.7 %copy-start.1 = (bf16[128,4096]{1,0:T(8,128)(2,1)S(1)}, bf16[128,4096]{1,0:T(8,128)(2,1)}, u32[]{:S(2)}) copy-start(bf16[128,4096]{1,0:T(8,128)(2,1)} %q_ref.5) | copy-start | bytes 3145732
  55.4 23.7 %copy-start.3 = (bf16[128,4096]{1,0:T(8,128)(2,1)S(1)}, bf16[128,4096]{1,0:T(8,128)(2,1)}, u32[]{:S(2)}) copy-start(bf16[128,4096]{1,0:T(8,128)(2,1)} %x_ref.5) | copy-start | bytes 3145732
  75.4 2.0 %collective-permute-start.15 = (bf16[1,64,4096]{2,1,0:T(8,128)(2,1)S(1)}, bf16[1,64,4096]{2,1,0:T(8,128)(2,1)S(1)}, u32[]{:S(2)}, u32[]{:S(2)}) collective-permute-start(bf16[1,64,4096]{2,1,0:T(8,128)(2,1)S(1)} %get-tuple-element.16), channel_id=1, source_target_pairs={{0,1},{1,0},{2,3},{3,2},{4,5},{5,4},{6,7},{7,6},{8,9},{9,8},{10,11... | collective-permute-start | bytes 1572872 | tf_op jit(solution)/shard_map/ppermute | solution.py:346
  77.5 16.0 %collective-permute-start.16 = (bf16[1,32,4096]{2,1,0:T(8,128)(2,1)S(1)}, bf16[1,32,4096]{2,1,0:T(8,128)(2,1)S(1)}, u32[]{:S(2)}, u32[]{:S(2)}) collective-permute-start(bf16[1,32,4096]{2,1,0:T(8,128)(2,1)S(1)} %slice.43), channel_id=1, source_target_pairs={{0,2},{1,3},{2,0},{3,1},{4,6},{5,7},{6,4},{7,5},{8,10},{9,11},{10,... | collective-permute-start | bytes 786440 | tf_op jit(solution)/shard_map/ppermute | solution.py:346
  93.6 18.3 %collective-permute-start.19 = (bf16[8,4096]{1,0:T(8,128)(2,1)S(1)}, bf16[8,4096]{1,0:T(8,128)(2,1)S(1)}, u32[]{:S(2)}, u32[]{:S(2)}) collective-permute-start(bf16[8,4096]{1,0:T(8,128)(2,1)S(1)} %get-tuple-element.17), channel_id=1, source_target_pairs={{0,12},{1,13},{2,14},{3,15},{4,0},{5,1},{6,2},{7,3},{8,4},{9,5},{1... | collective-permute-start | bytes 196616 | tf_op jit(solution)/shard_map/ppermute | solution.py:346
  93.7 18.3 %collective-permute-start.18 = (bf16[8,4096]{1,0:T(8,128)(2,1)S(1)}, bf16[8,4096]{1,0:T(8,128)(2,1)S(1)}, u32[]{:S(2)}, u32[]{:S(2)}) collective-permute-start(bf16[8,4096]{1,0:T(8,128)(2,1)S(1)} %get-tuple-element.18), channel_id=1, source_target_pairs={{0,8},{1,9},{2,10},{3,11},{4,12},{5,13},{6,14},{7,15},{8,0},{9,1},... | collective-permute-start | bytes 196616 | tf_op jit(solution)/shard_map/ppermute | solution.py:346
  93.7 18.2 %copy-start.7 = (s32[128,4]{0,1:T(4,128)S(1)}, s32[128,4]{0,1:T(4,128)}, u32[]{:S(2)}) copy-start(s32[128,4]{0,1:T(4,128)} %param.17) | copy-start | bytes 6148
  93.8 18.2 %copy-start.8 = (f32[128,4]{0,1:T(4,128)S(1)}, f32[128,4]{0,1:T(4,128)}, u32[]{:S(2)}) copy-start(f32[128,4]{0,1:T(4,128)} %param.18) | copy-start | bytes 6148
  93.8 18.2 %collective-permute-start.17 = (bf16[8,4096]{1,0:T(8,128)(2,1)S(1)}, bf16[8,4096]{1,0:T(8,128)(2,1)S(1)}, u32[]{:S(2)}, u32[]{:S(2)}) collective-permute-start(bf16[8,4096]{1,0:T(8,128)(2,1)S(1)} %get-tuple-element.19), channel_id=1, source_target_pairs={{0,4},{1,5},{2,6},{3,7},{4,8},{5,9},{6,10},{7,11},{8,12},{9,13},{1... | collective-permute-start | bytes 196616 | tf_op jit(solution)/shard_map/ppermute | solution.py:346
where the time goes:
time: 113 us; the launch traced here: 114 us
  Pallas kernels  51.3 us (45%)
  waiting for transfers between devices  38.5 us (34%)
  starting transfers between devices  13.7 us (12%)
  local copies, waits for them, and re-layouts  10 us (9%)
    ppermute x20, waiting for transfers between devices, move(): return lax.ppermute(value, 'expert', [(s, target(s)) for s in range(n)])  38.5 us
    pallas_call x2, Pallas kernels, local(): pl.pallas_call(functools.partial(own_kernel, n, h), out_shape=jax.ShapeDt...  28.9 us
    pallas_call x1, Pallas kernels, local(): pl.pallas_call(functools.partial(expert_kernel, n), out_shape=[half, half...  20 us
    ppermute x20, starting transfers between devices, move(): return lax.ppermute(value, 'expert', [(s, target(s)) for s in range(n)])  13.7 us
    unnamed x26, local copies, waits for them, and re-layouts  9.98 us
  transfers between devices with their start and end apart: 20, of which 7 were waited for; matrix products, arithmetic and copies ran while one was open for 0% of the time, Pallas kernels for 25%

commit v1 on v0

v1 whole, which is shorter than its diff:
```python
import functools
import math

import jax
import jax.numpy as jnp
from jax import lax
from jax.experimental import pallas as pl
from jax.experimental.pallas import tpu as pltpu
from jax.sharding import PartitionSpec as P

HEAD = 128
QUERY_HEADS = 32
KV_HEADS = 2
GROUP = QUERY_HEADS // KV_HEADS
SHARDS = 4
SLOTS = 8
TILE = 128
KEYS = 256
KV_ROWS = TILE + 16
SCALE = math.log2(math.e) / math.sqrt(HEAD)
LOW = -1e30
F32 = jnp.float32
BF16 = jnp.bfloat16
VMEM = pl.BlockSpec(memory_space=pltpu.VMEM)
SMEM = pl.BlockSpec(memory_space=pltpu.SMEM)
ANY = pl.BlockSpec(memory_space=pl.ANY)
HBM = pl.BlockSpec(memory_space=pltpu.HBM)


def dot(a, b, ca=1, cb=0):
    return lax.dot_general(a, b, (((ca,), (cb,)), ((), ())), preferred_element_type=F32)


def reach(n):
    longest = n * TILE // 2 + 256
    return (longest - 1 + TILE - 1) // TILE


def slot_rows(routes, experts):
    members = jnp.concatenate(
        [jnp.max((routes == e).astype(F32), axis=0, keepdims=True) for e in experts], axis=0
    )
    count = len(experts)
    padded = -(-count // 8) * 8
    wide = members
    if padded > count:
        wide = jnp.concatenate([members, jnp.zeros((padded - count, TILE), F32)], axis=0)
    before = lax.broadcasted_iota(jnp.int32, (TILE, TILE), 0) < lax.broadcasted_iota(
        jnp.int32, (TILE, TILE), 1
    )
    ranks = dot(wide.astype(BF16), before.astype(F32).astype(BF16))
    return members, ranks


def pack_kernel(docs_ref, keys_ref, values_ref, out_ref, docs, values, sems):
    moves = [
        pltpu.make_async_copy(values_ref, values, sems.at[0]),
        pltpu.make_async_copy(docs_ref, docs, sems.at[1]),
        pltpu.make_async_copy(
            keys_ref, out_ref.at[pl.ds(0, TILE), pl.ds(0, KV_HEADS * HEAD)], sems.at[2]
        ),
    ]
    for move in moves:
        move.start()
    moves[0].wait()
    for h in range(KV_HEADS):
        out_ref[0:TILE, (KV_HEADS + h) * HEAD : (KV_HEADS + h + 1) * HEAD] = (
            values[:, h * HEAD : (h + 1) * HEAD].astype(F32).T.astype(BF16)
        )
    moves[1].wait()
    out_ref[TILE:KV_ROWS, :] = jnp.zeros((KV_ROWS - TILE, 4 * HEAD), BF16)
    out_ref[TILE:KV_ROWS, 0:HEAD] = jnp.broadcast_to(
        docs[...].astype(F32), (KV_ROWS - TILE, TILE)
    ).astype(BF16)
    moves[2].wait()


def select_kernel(planes, pos_ref, routes_ref, docs_ref, q_ref, x_ref, qs_ref, xs_ref, facts_ref):
    z = pos_ref[0] // SHARDS
    members, ranks = slot_rows(routes_ref[...], [lax.rem(z + k, planes) for k in range(planes)])
    docs = docs_ref[...].astype(F32)
    lane_slot = (lax.broadcasted_iota(jnp.int32, (TILE, TILE), 0) % SLOTS).astype(F32)
    token = lax.broadcasted_iota(jnp.int32, (1, TILE), 1).astype(F32)
    facts = jnp.concatenate(
        [token, docs, jnp.ones((1, TILE), F32), jnp.zeros((5, TILE), F32)], axis=0
    ).astype(BF16)
    picks = [
        jnp.where(ranks[k : k + 1] == lane_slot, members[k : k + 1], 0.0) for k in range(planes)
    ]
    chooser = jnp.concatenate([p[:SLOTS] for p in picks], axis=0).astype(BF16)
    q_rows = dot(chooser, q_ref[...])
    xs_ref[...] = dot(chooser, x_ref[...])
    for k in range(planes):
        known = dot(facts, picks[k].astype(BF16), 1, 1)
        facts_ref[:, k * TILE : (k + 1) * TILE] = jnp.concatenate(
            [known[0:1], known[1:2] + (1.0 - known[2:3]) * docs[:, 0:1], known[2:]], axis=0
        )
        for h in range(KV_HEADS):
            for g in range(0, GROUP, 2):
                a = h * GROUP + g
                two = jnp.concatenate(
                    [
                        q_rows[k * SLOTS : (k + 1) * SLOTS, i * HEAD : (i + 1) * HEAD]
                        for i in (a, a + 1)
                    ],
                    axis=0,
                )
                at = k * TILE + g * SLOTS
                qs_ref[h, at : at + 2 * SLOTS, :] = two.astype(BF16)


def doc_starts(n, pos, held):
    sums = [jnp.zeros((1, TILE), F32) for _ in range(3)]
    for s in range(n):
        docs = held[s, TILE:KV_ROWS, 0:HEAD].astype(F32)[0:1]
        ahead = (pos - s < 0).astype(F32)
        behind = (pos - s > reach(n)).astype(F32)
        known = 1.0 - ahead - behind
        docs = jnp.where(known > 0.5, docs, 0.0) + 9.0 * ahead
        for d in range(3):
            sums[d] = sums[d] + jnp.where(docs < d + 1.0, 1.0, 0.0)
    return [jnp.sum(s, axis=1, keepdims=True) for s in sums]


def starts_of(docs, starts):
    first = jnp.zeros_like(docs)
    for d in range(3):
        first = jnp.where(docs == d + 1.0, starts[d], first)
    return first


def flash(pos, held, queries, kv_heads, acc_ref, bias_ref, place, first):
    lanes = place.shape[1]
    chains = len(queries)
    for i in range(chains):
        acc_ref[i] = jnp.zeros((HEAD, lanes), F32)
    low = jnp.min(first).astype(jnp.int32) // KEYS
    last = pos // (KEYS // TILE)
    clear = (jnp.max(first).astype(jnp.int32) + KEYS - 1) // KEYS
    middle = jnp.minimum(clear, last)

    def step(kb, carried, masked):
        if masked:
            key_at = (kb * KEYS + lax.broadcasted_iota(jnp.int32, (KEYS, 1), 0)).astype(F32)
            bias_ref[...] = jnp.where((key_at >= first) & (key_at <= place), 0.0, LOW)
        out = []
        for i in range(chains):
            top, total = carried[2 * i], carried[2 * i + 1]
            h = kv_heads[i]
            keys = jnp.concatenate(
                [held[2 * kb + t, 0:TILE, h * HEAD : (h + 1) * HEAD] for t in range(2)], axis=0
            )
            values = jnp.concatenate(
                [
                    held[2 * kb + t, 0:TILE, (KV_HEADS + h) * HEAD : (KV_HEADS + h + 1) * HEAD]
                    for t in range(2)
                ],
                axis=1,
            )
            scores = dot(keys, queries[i](), 1, 1)
            if masked:
                scores = scores + bias_ref[...]
            new_top = jnp.maximum(top, jnp.max(scores, axis=0, keepdims=True))
            factor = jnp.exp2((top - new_top) * SCALE)
            weights = jnp.exp2((scores - new_top) * SCALE)
            acc_ref[i] = acc_ref[i] * factor + dot(values, weights.astype(BF16))
            out += [new_top, total * factor + jnp.sum(weights, axis=0, keepdims=True)]
        return tuple(out)

    state = (jnp.full((1, lanes), LOW, F32), jnp.zeros((1, lanes), F32)) * chains
    state = lax.fori_loop(low, middle, functools.partial(step, masked=True), state)
    state = lax.fori_loop(middle, last, functools.partial(step, masked=False), state)
    state = step(last, state, True)
    return [(acc_ref[i] / state[2 * i + 1]).T for i in range(chains)]


def routed_kernel(n, senders, pos_ref, gain_ref, qs_ref, xs_ref, facts_ref, *refs):
    planes = n // SHARDS
    count = len(senders)
    pieces = refs[:count]
    outs = refs[count : count + planes]
    held = refs[count + planes]
    acc, bias, state, sems = refs[count + planes + 1 :]
    pos = pos_ref[0]
    z, y, c = pos // SHARDS, (pos // 2) % 2, pos % 2
    copies = []
    for i, (flip_c, flip_y, k) in enumerate(senders):
        sender = lax.rem(z - k + planes, planes) * SHARDS + (y ^ flip_y) * 2 + (c ^ flip_c)
        copies.append(pltpu.make_async_copy(pieces[i], held.at[sender], sems.at[i]))
    for copy in copies:
        copy.start()
    for copy in copies:
        copy.wait()
    starts = doc_starts(n, pos, held)
    lanes = 2 * TILE
    base = (pos * TILE).astype(F32)
    for part in range(planes // 2):
        at = part * lanes
        place = facts_ref[0:1, at : at + lanes] + base
        first = starts_of(facts_ref[1:2, at : at + lanes], starts)
        done = flash(
            pos,
            held,
            [lambda h=h, at=at: qs_ref[h, at : at + lanes, :] for h in range(KV_HEADS)],
            list(range(KV_HEADS)),
            acc,
            bias,
            place,
            first,
        )
        for h in range(KV_HEADS):
            for k in range(2):
                row = (part * 2 + k) * SLOTS
                for g in range(GROUP):
                    lane = (h * GROUP + g) * HEAD
                    state[row : row + SLOTS, lane : lane + HEAD] = (
                        xs_ref[row : row + SLOTS, lane : lane + HEAD]
                        + done[h][k * TILE + g * SLOTS : k * TILE + (g + 1) * SLOTS]
                    )
    for k in range(planes):
        hidden = state[k * SLOTS : (k + 1) * SLOTS, :]
        mean = jnp.mean(hidden * hidden, axis=1, keepdims=True)
        outs[k][...] = (hidden * lax.rsqrt(mean + 1e-06) * gain_ref[...]).astype(BF16)


def expert_kernel(count, *refs):
    pieces = refs[:count]
    weights = refs[count : count + 3]
    keep_ref, send_ref = refs[count + 3 : count + 5]
    wg, wu, wd, rows, sems = refs[count + 5 :]
    loads = [
        pltpu.make_async_copy(src.at[0], dst, sems.at[i])
        for i, (src, dst) in enumerate(zip(weights, (wg, wu, wd)))
    ]
    for load in loads:
        load.start()
    width = rows.shape[1]
    batch = min(count, 16)
    step = 1024
    for b in range(count // batch):
        for i in range(0, batch, 2):
            for col in range(0, width, step):
                rows[i * SLOTS : (i + 2) * SLOTS, col : col + step] = jnp.concatenate(
                    [pieces[b * batch + i + t][:, col : col + step].astype(F32) for t in range(2)],
                    axis=0,
                ).astype(BF16)
        if b == 0:
            loads[0].wait()
        gate = dot(rows[...], wg[...])
        if b == 0:
            loads[1].wait()
        up = dot(rows[...], wu[...])
        act = (gate / (1.0 + jnp.exp(-gate)) * up).astype(BF16)
        if b == 0:
            loads[2].wait()
        out_rows = batch * SLOTS
        for col in range(0, width, step):
            part = dot(act, wd[:, col : col + step]).astype(BF16)
            half = count * SLOTS // 2
            at = b * out_rows
            if out_rows > half:
                keep_ref[:, col : col + step] = part[:half]
                send_ref[:, col : col + step] = part[half:]
            elif at < half:
                keep_ref[at : at + out_rows, col : col + step] = part
            else:
                send_ref[at - half : at - half + out_rows, col : col + step] = part


def own_kernel(n, part, pos_ref, held, q_ref, x_ref, _, h_ref, acc, bias):
    pos = pos_ref[0]
    starts = doc_starts(n, pos, held)
    first = starts_of(held[pos, TILE:KV_ROWS, 0:HEAD].astype(F32)[0:1], starts)
    place = (pos * TILE + lax.broadcasted_iota(jnp.int32, (1, TILE), 1)).astype(F32)
    place = jnp.concatenate([place] * 2, axis=1)
    first = jnp.concatenate([first] * 2, axis=1)

    def rows(i):
        return jnp.concatenate(
            [q_ref[:, a * HEAD : (a + 1) * HEAD] for a in (2 * i, 2 * i + 1)], axis=0
        )

    done = flash(
        pos,
        held,
        [lambda i=i: rows(i) for i in range(4)],
        [part // 2] * 4,
        acc,
        bias,
        place,
        first,
    )
    for i in range(4):
        for g in range(2):
            lane = (2 * i + g) * HEAD
            h_ref[:, lane : lane + HEAD] = (
                x_ref[:, lane : lane + HEAD].astype(F32) + done[i][g * TILE : (g + 1) * TILE]
            )


def combine_kernel(planes, pos_ref, routes_ref, gates_ref, *refs):
    halves, parts, out_ref = refs[:4], refs[4 : 4 + planes], refs[4 + planes]
    z = pos_ref[0] // SHARDS
    routes = routes_ref[...]
    gates = gates_ref[...]
    experts = [lax.rem(z + k, planes) for k in range(planes)]
    members, ranks = slot_rows(routes, experts)
    slot = lax.broadcasted_iota(jnp.int32, (SLOTS, TILE), 0).astype(F32)
    mix = []
    for k, e in enumerate(experts):
        gate = jnp.sum(jnp.where(routes == e, gates, 0.0), axis=0, keepdims=True)
        mix.append(jnp.where(ranks[k : k + 1] == slot, gate, 0.0))
    mix = jnp.concatenate(mix, axis=0).T
    mix_high = mix.astype(BF16)
    mix_low = (mix - mix_high.astype(F32)).astype(BF16)
    size = halves[0].shape[1]
    for i, h in enumerate(halves):
        columns = slice(i * size, (i + 1) * size)
        rows = jnp.concatenate([p[:, columns].astype(F32) for p in parts], axis=0).astype(BF16)
        out_ref[:, columns] = (h[...] + dot(mix_high, rows) + dot(mix_low, rows)).astype(BF16)


def params(mib):
    return pltpu.CompilerParams(vmem_limit_bytes=mib * 1024 * 1024)


def local(
    resid, queries, keys, values, doc_ids, norm_gain, routes, route_weights, w_gate, w_up, w_down
):
    n = lax.axis_size("expert")
    planes = n // SHARDS
    pos = lax.axis_index("expert").astype(jnp.int32).reshape(1)
    tokens, width = queries.shape
    hidden = w_gate.shape[2]
    routes_t = routes.T
    gates_t = route_weights.T
    docs = doc_ids.reshape(1, tokens)
    small = 24 if n <= 16 else 60
    back = reach(n)

    packed = pl.pallas_call(
        pack_kernel,
        out_shape=jax.ShapeDtypeStruct((KV_ROWS, 4 * HEAD), BF16),
        in_specs=[HBM] * 3,
        out_specs=VMEM,
        scratch_shapes=[
            pltpu.VMEM((1, tokens), jnp.int32),
            pltpu.VMEM((tokens, KV_HEADS * HEAD), BF16),
            pltpu.SemaphoreType.DMA((3,)),
        ],
        compiler_params=params(small),
        name="pack",
    )(docs, keys, values)

    def move(value, pairs):
        return lax.ppermute(value, "expert", pairs)

    def needed(tile, devices):
        return any(tile <= t <= tile + back for t in devices)

    kv = {(0, 0, 0): packed}
    for k in range(1, planes):
        pairs = [
            (s, s + k * SHARDS)
            for s in range(n - k * SHARDS)
            if needed(s, [(s // SHARDS + k) * SHARDS + j for j in range(SHARDS)])
        ]
        if pairs:
            kv[0, 0, k] = move(packed, pairs)
    for (_, _, k), piece in list(kv.items()):
        pairs = [
            (d, d ^ 2)
            for d in range(n)
            if d >= k * SHARDS and needed(d - k * SHARDS, [d ^ 2, d ^ 3])
        ]
        if pairs:
            kv[0, 1, k] = move(piece, pairs)
    for (_, flip_y, k), piece in list(kv.items()):
        pairs = [
            (d, d ^ 1)
            for d in range(n)
            if d >= k * SHARDS and needed((d - k * SHARDS) ^ (2 * flip_y), [d ^ 1])
        ]
        if pairs:
            kv[1, flip_y, k] = move(piece, pairs)

    q_rows, x_rows, facts = pl.pallas_call(
        functools.partial(select_kernel, planes),
        out_shape=[
            jax.ShapeDtypeStruct((KV_HEADS, planes * TILE, HEAD), BF16),
            jax.ShapeDtypeStruct((planes * SLOTS, width), F32),
            jax.ShapeDtypeStruct((8, planes * TILE), F32),
        ],
        in_specs=[SMEM] + [VMEM] * 4,
        out_specs=[VMEM] * 3,
        compiler_params=params(small),
        name="select",
    )(pos, routes_t, docs, queries, resid)

    *sent, held = pl.pallas_call(
        functools.partial(routed_kernel, n, list(kv)),
        out_shape=[jax.ShapeDtypeStruct((SLOTS, width), BF16)] * planes
        + [jax.ShapeDtypeStruct((n, KV_ROWS, 4 * HEAD), BF16)],
        in_specs=[SMEM] + [VMEM] * 4 + [ANY] * len(kv),
        out_specs=[VMEM] * (planes + 1),
        scratch_shapes=[
            pltpu.VMEM((KV_HEADS, HEAD, 2 * TILE), F32),
            pltpu.VMEM((KEYS, 2 * TILE), F32),
            pltpu.VMEM((planes * SLOTS, width), F32),
            pltpu.SemaphoreType.DMA((len(kv),)),
        ],
        compiler_params=params(small),
        name="routed",
    )(pos, norm_gain.reshape(1, width), q_rows, x_rows, facts, *kv.values())

    def own(part, after):
        columns = pl.BlockSpec((tokens, 8 * HEAD), lambda i: (0, part))
        return pl.pallas_call(
            functools.partial(own_kernel, n, part),
            out_shape=jax.ShapeDtypeStruct((tokens, 8 * HEAD), F32),
            grid=(1,),
            in_specs=[SMEM, VMEM, columns, columns, ANY],
            out_specs=pl.BlockSpec((tokens, 8 * HEAD), lambda i: (0, 0)),
            scratch_shapes=[
                pltpu.VMEM((4, HEAD, 2 * TILE), F32),
                pltpu.VMEM((KEYS, 2 * TILE), F32),
            ],
            compiler_params=params(small),
            cost_estimate=pl.CostEstimate(
                flops=2_000_000_000, bytes_accessed=8_000_000, transcendentals=2_000_000
            ),
            name="own",
        )(pos, held, queries, resid, after)

    halves = [own(part, sent[0]) for part in range(2)]

    pieces = [sent[0]]
    for k in range(1, planes):
        pieces.append(move(sent[k], [(s, (s + k * SHARDS) % n) for s in range(n)]))
    pieces += [move(p, [(s, s ^ 2) for s in range(n)]) for p in pieces]
    pieces += [move(p, [(s, s ^ 1) for s in range(n)]) for p in pieces]

    half = jax.ShapeDtypeStruct((n * SLOTS // 2, width), BF16)
    keep, send = pl.pallas_call(
        functools.partial(expert_kernel, n),
        out_shape=[half, half],
        in_specs=[VMEM] * n + [HBM] * 3,
        out_specs=[VMEM, VMEM],
        scratch_shapes=[
            pltpu.VMEM((width, hidden), BF16),
            pltpu.VMEM((width, hidden), BF16),
            pltpu.VMEM((hidden, width), BF16),
            pltpu.VMEM((16 * SLOTS, width), BF16),
            pltpu.SemaphoreType.DMA((3,)),
        ],
        compiler_params=params(small),
        cost_estimate=pl.CostEstimate(
            flops=1_200_000_000, bytes_accessed=12_000_000, transcendentals=50_000
        ),
        name="expert",
    )(*pieces, w_gate, w_up, w_down)

    halves += [own(part, keep) for part in range(2, 4)]

    total = keep.astype(F32) + move(send, [(s, s ^ 1) for s in range(n)]).astype(F32)
    quarter = n * SLOTS // 4
    other = move(total[quarter:].astype(BF16), [(s, s ^ 2) for s in range(n)])
    total = (total[:quarter] + other.astype(F32)).astype(BF16)
    parts = [total[:SLOTS]]
    for k in range(1, planes):
        parts.append(
            move(
                total[k * SLOTS : (k + 1) * SLOTS], [(s, (s - k * SHARDS) % n) for s in range(n)]
            )
        )

    return pl.pallas_call(
        functools.partial(combine_kernel, planes),
        out_shape=jax.ShapeDtypeStruct((tokens, width), BF16),
        in_specs=[SMEM] + [VMEM] * (6 + planes),
        out_specs=VMEM,
        compiler_params=params(small),
        name="combine",
    )(pos, routes_t, gates_t, *halves, *parts)


def solution(mesh):
    rows = P(("groups", "expert"), None)
    in_specs = (rows,) * 4 + (P(("groups", "expert")), P(), rows, rows) + (
        P("expert", None, None),
    ) * 3
    return jax.shard_map(local, mesh=mesh, in_specs=in_specs, out_specs=rows, check_vma=False)
```

time: 113 us -> 118 us (1.044)
  waiting for transfers between devices: 38.5 us -> 16.2 us
  starting transfers between devices: 13.7 us -> 35.5 us
  local copies, waits for them, and re-layouts: 10 us -> 15.5 us
    ppermute x20 -> x34, waiting for transfers between devices: 38.5 us -> 16.2 us  [move(): return lax.ppermute(value, 'expert', pairs)]
    ppermute x20 -> x34, starting transfers between devices: 13.7 us -> 35.5 us  [move(): return lax.ppermute(value, 'expert', pairs)]
    pallas_call x1, Pallas kernels: 20 us -> 2.87 us  [local(): pl.pallas_call(functools.partial(expert_kernel, n), out_shape=[half, half...]
    pallas_call x3 -> x7, Pallas kernels: 29.5 us -> 45.6 us  [the longest x4 33.1 us: own(): pl.pallas_call(functools.partial(own_kernel, n, part), out_shape=jax.Shap...]
    unnamed x26 -> x42, local copies, waits for them, and re-layouts: 9.98 us -> 15.4 us
  transfers between devices with their start and end apart: 20 -> 34, of which waited for: 7 -> 8; matrix products, arithmetic and copies ran while one was open for 0% -> 0% of each run, Pallas kernels for 25% -> 29%
where the time goes in v1:
time: 118 us
  Pallas kernels  50.3 us (43%)
  starting transfers between devices  35.5 us (30%)
  waiting for transfers between devices  16.2 us (14%)
  local copies, waits for them, and re-layouts  15.5 us (13%)
    ppermute x34, starting transfers between devices, move(): return lax.ppermute(value, 'expert', pairs)  35.5 us
    pallas_call x4, Pallas kernels, own(): pl.pallas_call(functools.partial(own_kernel, n, part), out_shape=jax.Shap...  33.1 us
    ppermute x34, waiting for transfers between devices, move(): return lax.ppermute(value, 'expert', pairs)  16.2 us
    unnamed x42, local copies, waits for them, and re-layouts  15.4 us
    pallas_call x1, Pallas kernels, local(): pl.pallas_call(functools.partial(routed_kernel, n, list(kv)), out_shape=[...  11.7 us
    pallas_call x1, Pallas kernels, local(): pl.pallas_call(functools.partial(expert_kernel, n), out_shape=[half, half...  2.87 us
  transfers between devices with their start and end apart: 34, of which 8 were waited for; matrix products, arithmetic and copies ran while one was open for 0% of the time, Pallas kernels for 29%

profile of v1, /device:TPU:26, one launch (start us, length us, event | category | flops | bytes accessed | tf_op | source)
XLA Modules:
  0.0 118.2 jit_solution(11240054058943524526)
XLA Ops:
  0.0 1.0 copy-done.13
  1.0 0.8 copy-done.14
  1.8 0.7 copy-done.18
  2.7 3.4 %collective-permute-start.3 = (bf16[144,512]{1,0:T(8,128)(2,1)S(1)}, bf16[144,512]{1,0:T(8,128)(2,1)S(1)}, u32[]{:S(2)}, u32[]{:S(2)}) collective-permute-start(bf16[144,512]{1,0:T(8,128)(2,1)S(1)} %pack.1.refs_0_), channel_id=1, source_target_pairs={{0,2},{1,3},{4,6},{5,7},{8,10},{9,11},{12,14},{13,15},{16,18},{17,... | collective-permute-start | bytes 442376 | tf_op jit(solution)/shard_map/ppermute | solution.py:356
  6.1 0.7 collective-permute-start.2
  6.8 1.3 %collective-permute-start.1 = (bf16[144,512]{1,0:T(8,128)(2,1)S(1)}, bf16[144,512]{1,0:T(8,128)(2,1)}, u32[]{:S(2)}, u32[]{:S(2)}) collective-permute-start(bf16[144,512]{1,0:T(8,128)(2,1)S(1)} %pack.1.refs_0_), channel_id=1, source_target_pairs={{0,8},{1,9},{2,10},{3,11},{4,12},{5,13},{6,14},{7,15},{16,24},{17,... | collective-permute-start | bytes 442376 | tf_op jit(solution)/shard_map/ppermute | solution.py:356
  8.1 1.3 %collective-permute-start = (bf16[144,512]{1,0:T(8,128)(2,1)S(1)}, bf16[144,512]{1,0:T(8,128)(2,1)}, u32[]{:S(2)}, u32[]{:S(2)}) collective-permute-start(bf16[144,512]{1,0:T(8,128)(2,1)S(1)} %pack.1.refs_0_), channel_id=1, source_target_pairs={{0,4},{1,5},{2,6},{3,7},{4,8},{5,9},{6,10},{7,11},{8,12},{9,13},{1... | collective-permute-start | bytes 442376 | tf_op jit(solution)/shard_map/ppermute | solution.py:356
  9.4 1.5 %collective-permute-start.7 = (bf16[144,512]{1,0:T(8,128)(2,1)S(1)}, bf16[144,512]{1,0:T(8,128)(2,1)S(1)}, u32[]{:S(2)}, u32[]{:S(2)}) collective-permute-start(bf16[144,512]{1,0:T(8,128)(2,1)S(1)} %pack.1.refs_0_), channel_id=1, source_target_pairs={{0,1},{2,3},{4,5},{6,7},{8,9},{10,11},{12,13},{14,15},{16,17},{18,... | collective-permute-start | bytes 442376 | tf_op jit(solution)/shard_map/ppermute | solution.py:356
  10.9 0.7 collective-permute-start.10
  11.6 1.3 %collective-permute-start.6 = (bf16[144,512]{1,0:T(8,128)(2,1)S(1)}, bf16[144,512]{1,0:T(8,128)(2,1)}, u32[]{:S(2)}, u32[]{:S(2)}) collective-permute-start(bf16[144,512]{1,0:T(8,128)(2,1)S(1)} %collective-permute-done.2.refs_3_), channel_id=1, source_target_pairs={{14,12},{15,13},{30,28},{31,29}} | collective-permute-start | bytes 442376 | tf_op jit(solution)/shard_map/ppermute | solution.py:356
  12.9 0.7 copy-done.7
  13.5 4.7 %collective-permute-done.1.refs_2_ = bf16[144,512]{1,0:T(8,128)(2,1)} collective-permute-done((bf16[144,512]{1,0:T(8,128)(2,1)S(1)}, bf16[144,512]{1,0:T(8,128)(2,1)}, u32[]{:S(2)}, u32[]{:S(2)}) %collective-permute-start.1) | collective-permute-done | bytes 147488 | tf_op jit(solution)/shard_map/ppermute | solution.py:356
  18.2 5.0 %collective-permute-start.5 = (bf16[144,512]{1,0:T(8,128)(2,1)}, bf16[144,512]{1,0:T(8,128)(2,1)}, u32[]{:S(2)}, u32[]{:S(2)}) collective-permute-start(bf16[144,512]{1,0:T(8,128)(2,1)} %collective-permute-done.1.refs_2_), channel_id=1, source_target_pairs={{8,10},{9,11},{10,8},{11,9},{12,14},{13,15},{14,12},{15,13},{24,26... | collective-permute-start | bytes 442376 | tf_op jit(solution)/shard_map/ppermute | solution.py:356
  23.2 1.9 %collective-permute-start.4 = (bf16[144,512]{1,0:T(8,128)(2,1)}, bf16[144,512]{1,0:T(8,128)(2,1)}, u32[]{:S(2)}, u32[]{:S(2)}) collective-permute-start(bf16[144,512]{1,0:T(8,128)(2,1)} %collective-permute-done.refs_1_), channel_id=1, source_target_pairs={{4,6},{5,7},{6,4},{7,5},{8,10},{9,11},{10,8},{11,9},{12,14},{13,15... | collective-permute-start | bytes 442376 | tf_op jit(solution)/shard_map/ppermute | solution.py:356
  25.2 0.6 copy-done.9
  25.8 1.9 %collective-permute-start.9 = (bf16[144,512]{1,0:T(8,128)(2,1)}, bf16[144,512]{1,0:T(8,128)(2,1)}, u32[]{:S(2)}, u32[]{:S(2)}) collective-permute-start(bf16[144,512]{1,0:T(8,128)(2,1)} %collective-permute-done.1.refs_2_), channel_id=1, source_target_pairs={{8,9},{9,8},{10,11},{11,10},{12,13},{13,12},{14,15},{15,14},{24,25... | collective-permute-start | bytes 442376 | tf_op jit(solution)/shard_map/ppermute | solution.py:356
  27.8 0.6 copy-done.11
  28.4 2.4 %collective-permute-start.8 = (bf16[144,512]{1,0:T(8,128)(2,1)}, bf16[144,512]{1,0:T(8,128)(2,1)}, u32[]{:S(2)}, u32[]{:S(2)}) collective-permute-start(bf16[144,512]{1,0:T(8,128)(2,1)} %collective-permute-done.refs_1_), channel_id=1, source_target_pairs={{4,5},{5,4},{6,7},{7,6},{8,9},{9,8},{10,11},{11,10},{12,13},{13,12... | collective-permute-start | bytes 442376 | tf_op jit(solution)/shard_map/ppermute | solution.py:356
  30.8 1.3 %collective-permute-start.13 = (bf16[144,512]{1,0:T(8,128)(2,1)}, bf16[144,512]{1,0:T(8,128)(2,1)}, u32[]{:S(2)}, u32[]{:S(2)}) collective-permute-start(bf16[144,512]{1,0:T(8,128)(2,1)} %collective-permute-done.6.refs_7_), channel_id=1, source_target_pairs={{13,12},{29,28}} | collective-permute-start | bytes 442376 | tf_op jit(solution)/shard_map/ppermute | solution.py:356
  32.1 3.7 %collective-permute-start.12 = (bf16[144,512]{1,0:T(8,128)(2,1)}, bf16[144,512]{1,0:T(8,128)(2,1)}, u32[]{:S(2)}, u32[]{:S(2)}) collective-permute-start(bf16[144,512]{1,0:T(8,128)(2,1)} %collective-permute-done.5.refs_6_), channel_id=1, source_target_pairs={{8,9},{9,8},{11,10},{12,13},{13,12},{15,14},{24,25},{25,24},{27,26... | collective-permute-start | bytes 442376 | tf_op jit(solution)/shard_map/ppermute | solution.py:356
  35.8 1.9 %collective-permute-start.11 = (bf16[144,512]{1,0:T(8,128)(2,1)}, bf16[144,512]{1,0:T(8,128)(2,1)}, u32[]{:S(2)}, u32[]{:S(2)}) collective-permute-start(bf16[144,512]{1,0:T(8,128)(2,1)} %collective-permute-done.4.refs_5_), channel_id=1, source_target_pairs={{4,5},{5,4},{6,7},{7,6},{8,9},{9,8},{10,11},{11,10},{12,13},{13,12... | collective-permute-start | bytes 442376 | tf_op jit(solution)/shard_map/ppermute | solution.py:356
  37.8 1.2 %copy-done.3 = bf16[128,4096]{1,0:T(8,128)(2,1)S(1)} copy-done((bf16[128,4096]{1,0:T(8,128)(2,1)S(1)}, bf16[128,4096]{1,0:T(8,128)(2,1)}, u32[]{:S(2)}) %copy-start.3) | copy-done | bytes 1048600
  39.0 1.2 %copy-done.5 = bf16[128,4096]{1,0:T(8,128)(2,1)S(1)} copy-done((bf16[128,4096]{1,0:T(8,128)(2,1)S(1)}, bf16[128,4096]{1,0:T(8,128)(2,1)}, u32[]{:S(2)}) %copy-start.5) | copy-done | bytes 1048600
  40.2 0.7 copy-done.16
  40.9 0.7 copy-done.19
  41.5 0.6 select.1
  42.2 0.9 copy-done.8
  43.1 0.9 copy-done.10
  44.0 0.9 copy-done.12
  44.9 0.7 copy-done.15
  45.6 11.7 %routed.1 = (bf16[8,4096]{1,0:T(8,128)(2,1)S(1)}, bf16[8,4096]{1,0:T(8,128)(2,1)S(1)}, bf16[8,4096]{1,0:T(8,128)(2,1)S(1)}, bf16[8,4096]{1,0:T(8,128)(2,1)S(1)}, bf16[16,144,512]{2,1,0:T(8,128)(2,1)S(1)}) custom-call(s32[1]{0:T(128)} %bitcast.pos_ref, f32[1,4096]{1,0:T(1,128)S(1)} %bitcast.5, bf16[2,512,128]{2,1,0:T(8,128)(2,1)S(1)} %get-tuple-element.15.qs_ref, ...), custom_call_target="tpu_custom_call" | custom-call | tf_op jit(solution)/shard_map/routed/pallas_call | solution.py:400
  57.5 1.9 %collective-permute-start.16 = (bf16[8,4096]{1,0:T(8,128)(2,1)S(1)}, bf16[8,4096]{1,0:T(8,128)(2,1)S(1)}, u32[]{:S(2)}, u32[]{:S(2)}) collective-permute-start(bf16[8,4096]{1,0:T(8,128)(2,1)S(1)} %get-tuple-element.22), channel_id=1, source_target_pairs={{0,12},{1,13},{2,14},{3,15},{4,0},{5,1},{6,2},{7,3},{8,4},{9,5},{1... | collective-permute-start | bytes 196616 | tf_op jit(solution)/shard_map/ppermute | solution.py:356
  59.4 3.6 %collective-permute-done.14.refs_1_ = bf16[8,4096]{1,0:T(8,128)(2,1)S(1)} collective-permute-done((bf16[8,4096]{1,0:T(8,128)(2,1)S(1)}, bf16[8,4096]{1,0:T(8,128)(2,1)S(1)}, u32[]{:S(2)}, u32[]{:S(2)}) %collective-permute-start.14) | collective-permute-done | bytes 65568 | tf_op jit(solution)/shard_map/ppermute | solution.py:356
  63.0 2.7 %collective-permute-done.15.refs_2_ = bf16[8,4096]{1,0:T(8,128)(2,1)S(1)} collective-permute-done((bf16[8,4096]{1,0:T(8,128)(2,1)S(1)}, bf16[8,4096]{1,0:T(8,128)(2,1)S(1)}, u32[]{:S(2)}, u32[]{:S(2)}) %collective-permute-start.15) | collective-permute-done | bytes 65568 | tf_op jit(solution)/shard_map/ppermute | solution.py:356
  65.7 2.1 %collective-permute-start.19 = (bf16[8,4096]{1,0:T(8,128)(2,1)S(1)}, bf16[8,4096]{1,0:T(8,128)(2,1)S(1)}, u32[]{:S(2)}, u32[]{:S(2)}) collective-permute-start(bf16[8,4096]{1,0:T(8,128)(2,1)S(1)} %collective-permute-done.15.refs_2_), channel_id=1, source_target_pairs={{0,2},{1,3},{2,0},{3,1},{4,6},{5,7},{6,4},{7,5},{8,10},{9,11},{10,... | collective-permute-start | bytes 196616 | tf_op jit(solution)/shard_map/ppermute | solution.py:356
  68.0 2.4 %collective-permute-done.18.refs_5_ = bf16[8,4096]{1,0:T(8,128)(2,1)S(1)} collective-permute-done((bf16[8,4096]{1,0:T(8,128)(2,1)S(1)}, bf16[8,4096]{1,0:T(8,128)(2,1)S(1)}, u32[]{:S(2)}, u32[]{:S(2)}) %collective-permute-start.18) | collective-permute-done | bytes 65568 | tf_op jit(solution)/shard_map/ppermute | solution.py:356
  71.0 0.8 collective-permute-done.19.refs_6_
  71.8 0.8 collective-permute-done.20.refs_7_
  73.0 0.8 collective-permute-done.28.refs_15_
  73.8 1.9 %copy-done.1 = bf16[1,4096,384]{2,1,0:T(8,128)(2,1)S(1)} copy-done((bf16[1,4096,384]{2,1,0:T(8,128)(2,1)S(1)}, bf16[1,4096,384]{2,1,0:T(8,128)(2,1)}, u32[]{:S(2)}) %copy-start.1) | copy-done | bytes 3145752
  75.7 1.9 %copy-done.2 = bf16[1,384,4096]{2,1,0:T(8,128)(2,1)S(1)} copy-done((bf16[1,384,4096]{2,1,0:T(8,128)(2,1)S(1)}, bf16[1,384,4096]{2,1,0:T(8,128)(2,1)}, u32[]{:S(2)}) %copy-start.2) | copy-done | bytes 3145752
  77.6 2.9 %expert.1 = (bf16[64,4096]{1,0:T(8,128)(2,1)S(1)}, bf16[64,4096]{1,0:T(8,128)(2,1)S(1)}) custom-call(bf16[8,4096]{1,0:T(8,128)(2,1)S(1)} %get-tuple-element.19._.refs_0_, bf16[8,4096]{1,0:T(8,128)(2,1)S(1)} %collective-permute-done.14.refs_1_, bf16[8,4096]{1,0:T(8,128)(2,1)S(1)} %collective-permute-done.15.refs_2_, ...), custom_call_target="tpu_custom_call" | custom-call | flops 1200000000 | bytes 12000000 | tf_op jit(solution)/shard_map/expert/pallas_call | solution.py:444
  80.7 8.2 %own.5.refs_1_ = f32[128,1024]{1,0:T(8,128)S(1)} custom-call(s32[1]{0:T(128)} %bitcast.pos_ref, bf16[16,144,512]{2,1,0:T(8,128)(2,1)S(1)} %get-tuple-element.18.held, bf16[128,4096]{1,0:T(8,128)(2,1)S(1)} %copy-done.4, bf16[128,4096]{1,0:T(8,128)(2,1)S(1)} %copy-done.6, bf16[8,4096]{1,0:T(8,128)(2,1)S(1)} %get-tuple-element.19._.refs_0_), custom_call_target="tpu_custom_call" | custom-call | flops 2000000000 | bytes 8000000 | tf_op jit(solution)/shard_map/own/pallas_call | solution.py:418
  89.2 8.4 %own.4.refs_0_ = f32[128,1024]{1,0:T(8,128)S(1)} custom-call(s32[1]{0:T(128)} %bitcast.pos_ref, bf16[16,144,512]{2,1,0:T(8,128)(2,1)S(1)} %get-tuple-element.18.held, bf16[128,4096]{1,0:T(8,128)(2,1)S(1)} %copy-done.4, bf16[128,4096]{1,0:T(8,128)(2,1)S(1)} %copy-done.6, bf16[8,4096]{1,0:T(8,128)(2,1)S(1)} %get-tuple-element.19._.refs_0_), custom_call_target="tpu_custom_call" | custom-call | flops 2000000000 | bytes 8000000 | tf_op jit(solution)/shard_map/own/pallas_call | solution.py:418
  97.6 8.2 %own.7.refs_3_ = f32[128,1024]{1,0:T(8,128)S(1)} custom-call(s32[1]{0:T(128)} %bitcast.pos_ref, bf16[16,144,512]{2,1,0:T(8,128)(2,1)S(1)} %get-tuple-element.18.held, bf16[128,4096]{1,0:T(8,128)(2,1)S(1)} %copy-done.4, bf16[128,4096]{1,0:T(8,128)(2,1)S(1)} %copy-done.6, bf16[64,4096]{1,0:T(8,128)(2,1)S(1)} %get-tuple-element.23._), custom_call_target="tpu_custom_call" | custom-call | flops 2000000000 | bytes 8000000 | tf_op jit(solution)/shard_map/own/pallas_call | solution.py:418
  106.1 1.9 %collective-permute-start.31 = (bf16[8,4096]{1,0:T(8,128)(2,1)S(1)}, bf16[8,4096]{1,0:T(8,128)(2,1)S(1)}, u32[]{:S(2)}, u32[]{:S(2)}) collective-permute-start(bf16[8,4096]{1,0:T(8,128)(2,1)S(1)} %get-tuple-element.27), channel_id=1, source_target_pairs={{0,12},{1,13},{2,14},{3,15},{4,0},{5,1},{6,2},{7,3},{8,4},{9,5},{1... | collective-permute-start | bytes 196616 | tf_op jit(solution)/shard_map/ppermute | solution.py:356
  108.1 8.2 %own.6.refs_2_ = f32[128,1024]{1,0:T(8,128)S(1)} custom-call(s32[1]{0:T(128)} %bitcast.pos_ref, bf16[16,144,512]{2,1,0:T(8,128)(2,1)S(1)} %get-tuple-element.18.held, bf16[128,4096]{1,0:T(8,128)(2,1)S(1)} %copy-done.4, bf16[128,4096]{1,0:T(8,128)(2,1)S(1)} %copy-done.6, bf16[64,4096]{1,0:T(8,128)(2,1)S(1)} %get-tuple-element.23._), custom_call_target="tpu_custom_call" | custom-call | flops 2000000000 | bytes 8000000 | tf_op jit(solution)/shard_map/own/pallas_call | solution.py:418
  116.3 1.9 %combine.1 = bf16[128,4096]{1,0:T(8,128)(2,1)} custom-call(s32[1]{0:T(128)} %bitcast.pos_ref, s32[4,128]{1,0:T(4,128)S(1)} %bitcast.7, f32[4,128]{1,0:T(4,128)S(1)} %bitcast.10, f32[128,1024]{1,0:T(8,128)S(1)} %own.4.refs_0_, f32[128,1024]{1,0:T(8,128)S(1)} %own.5.refs_1_, f32[128,1024]{1,0:T(8,128)S(1)} %own.6.refs_2_, f32[128,1024]{1,0:T(8,128)S(1)} %own.7.refs_3_, ...), custom_call_target="tpu_custom_call" | custom-call | tf_op jit(solution)/shard_map/combine/pallas_call | solution.py:477
  (75 shorter events, 2.3 us)
Async XLA Ops:
  0.0 73.8 %copy-start = (bf16[1,4096,384]{2,1,0:T(8,128)(2,1)S(1)}, bf16[1,4096,384]{2,1,0:T(8,128)(2,1)}, u32[]{:S(2)}) copy-start(bf16[1,4096,384]{2,1,0:T(8,128)(2,1)} %refs_16_.1) | copy-start | bytes 9437188
  0.0 1.0 copy-start.13
  1.0 0.8 copy-start.14
  2.7 8.2 %collective-permute-start.3 = (bf16[144,512]{1,0:T(8,128)(2,1)S(1)}, bf16[144,512]{1,0:T(8,128)(2,1)S(1)}, u32[]{:S(2)}, u32[]{:S(2)}) collective-permute-start(bf16[144,512]{1,0:T(8,128)(2,1)S(1)} %pack.1.refs_0_), channel_id=1, source_target_pairs={{0,2},{1,3},{4,6},{5,7},{8,10},{9,11},{12,14},{13,15},{16,18},{17,... | collective-permute-start | bytes 442376 | tf_op jit(solution)/shard_map/ppermute | solution.py:356
  6.1 5.4 %collective-permute-start.2 = (bf16[144,512]{1,0:T(8,128)(2,1)S(1)}, bf16[144,512]{1,0:T(8,128)(2,1)S(1)}, u32[]{:S(2)}, u32[]{:S(2)}) collective-permute-start(bf16[144,512]{1,0:T(8,128)(2,1)S(1)} %pack.1.refs_0_), channel_id=1, source_target_pairs={{2,14},{3,15},{18,30},{19,31}} | collective-permute-start | bytes 442376 | tf_op jit(solution)/shard_map/ppermute | solution.py:356
  6.8 11.4 %collective-permute-start.1 = (bf16[144,512]{1,0:T(8,128)(2,1)S(1)}, bf16[144,512]{1,0:T(8,128)(2,1)}, u32[]{:S(2)}, u32[]{:S(2)}) collective-permute-start(bf16[144,512]{1,0:T(8,128)(2,1)S(1)} %pack.1.refs_0_), channel_id=1, source_target_pairs={{0,8},{1,9},{2,10},{3,11},{4,12},{5,13},{6,14},{7,15},{16,24},{17,... | collective-permute-start | bytes 442376 | tf_op jit(solution)/shard_map/ppermute | solution.py:356
  8.1 15.1 %collective-permute-start = (bf16[144,512]{1,0:T(8,128)(2,1)S(1)}, bf16[144,512]{1,0:T(8,128)(2,1)}, u32[]{:S(2)}, u32[]{:S(2)}) collective-permute-start(bf16[144,512]{1,0:T(8,128)(2,1)S(1)} %pack.1.refs_0_), channel_id=1, source_target_pairs={{0,4},{1,5},{2,6},{3,7},{4,8},{5,9},{6,10},{7,11},{8,12},{9,13},{1... | collective-permute-start | bytes 442376 | tf_op jit(solution)/shard_map/ppermute | solution.py:356
  9.4 15.7 %collective-permute-start.7 = (bf16[144,512]{1,0:T(8,128)(2,1)S(1)}, bf16[144,512]{1,0:T(8,128)(2,1)S(1)}, u32[]{:S(2)}, u32[]{:S(2)}) collective-permute-start(bf16[144,512]{1,0:T(8,128)(2,1)S(1)} %pack.1.refs_0_), channel_id=1, source_target_pairs={{0,1},{2,3},{4,5},{6,7},{8,9},{10,11},{12,13},{14,15},{16,17},{18,... | collective-permute-start | bytes 442376 | tf_op jit(solution)/shard_map/ppermute | solution.py:356
  10.9 16.8 %collective-permute-start.10 = (bf16[144,512]{1,0:T(8,128)(2,1)S(1)}, bf16[144,512]{1,0:T(8,128)(2,1)S(1)}, u32[]{:S(2)}, u32[]{:S(2)}) collective-permute-start(bf16[144,512]{1,0:T(8,128)(2,1)S(1)} %collective-permute-done.3.refs_4_), channel_id=1, source_target_pairs={{2,3},{3,2},{6,7},{7,6},{10,11},{11,10},{14,15},{15,14},{18,19},{1... | collective-permute-start | bytes 442376 | tf_op jit(solution)/shard_map/ppermute | solution.py:356
  11.6 19.2 %collective-permute-start.6 = (bf16[144,512]{1,0:T(8,128)(2,1)S(1)}, bf16[144,512]{1,0:T(8,128)(2,1)}, u32[]{:S(2)}, u32[]{:S(2)}) collective-permute-start(bf16[144,512]{1,0:T(8,128)(2,1)S(1)} %collective-permute-done.2.refs_3_), channel_id=1, source_target_pairs={{14,12},{15,13},{30,28},{31,29}} | collective-permute-start | bytes 442376 | tf_op jit(solution)/shard_map/ppermute | solution.py:356
  18.2 13.9 %collective-permute-start.5 = (bf16[144,512]{1,0:T(8,128)(2,1)}, bf16[144,512]{1,0:T(8,128)(2,1)}, u32[]{:S(2)}, u32[]{:S(2)}) collective-permute-start(bf16[144,512]{1,0:T(8,128)(2,1)} %collective-permute-done.1.refs_2_), channel_id=1, source_target_pairs={{8,10},{9,11},{10,8},{11,9},{12,14},{13,15},{14,12},{15,13},{24,26... | collective-permute-start | bytes 442376 | tf_op jit(solution)/shard_map/ppermute | solution.py:356
  23.2 12.6 %collective-permute-start.4 = (bf16[144,512]{1,0:T(8,128)(2,1)}, bf16[144,512]{1,0:T(8,128)(2,1)}, u32[]{:S(2)}, u32[]{:S(2)}) collective-permute-start(bf16[144,512]{1,0:T(8,128)(2,1)} %collective-permute-done.refs_1_), channel_id=1, source_target_pairs={{4,6},{5,7},{6,4},{7,5},{8,10},{9,11},{10,8},{11,9},{12,14},{13,15... | collective-permute-start | bytes 442376 | tf_op jit(solution)/shard_map/ppermute | solution.py:356
  25.8 16.3 %collective-permute-start.9 = (bf16[144,512]{1,0:T(8,128)(2,1)}, bf16[144,512]{1,0:T(8,128)(2,1)}, u32[]{:S(2)}, u32[]{:S(2)}) collective-permute-start(bf16[144,512]{1,0:T(8,128)(2,1)} %collective-permute-done.1.refs_2_), channel_id=1, source_target_pairs={{8,9},{9,8},{10,11},{11,10},{12,13},{13,12},{14,15},{15,14},{24,25... | collective-permute-start | bytes 442376 | tf_op jit(solution)/shard_map/ppermute | solution.py:356
  28.4 13.7 %collective-permute-start.8 = (bf16[144,512]{1,0:T(8,128)(2,1)}, bf16[144,512]{1,0:T(8,128)(2,1)}, u32[]{:S(2)}, u32[]{:S(2)}) collective-permute-start(bf16[144,512]{1,0:T(8,128)(2,1)} %collective-permute-done.refs_1_), channel_id=1, source_target_pairs={{4,5},{5,4},{6,7},{7,6},{8,9},{9,8},{10,11},{11,10},{12,13},{13,12... | collective-permute-start | bytes 442376 | tf_op jit(solution)/shard_map/ppermute | solution.py:356
  30.8 11.3 %collective-permute-start.13 = (bf16[144,512]{1,0:T(8,128)(2,1)}, bf16[144,512]{1,0:T(8,128)(2,1)}, u32[]{:S(2)}, u32[]{:S(2)}) collective-permute-start(bf16[144,512]{1,0:T(8,128)(2,1)} %collective-permute-done.6.refs_7_), channel_id=1, source_target_pairs={{13,12},{29,28}} | collective-permute-start | bytes 442376 | tf_op jit(solution)/shard_map/ppermute | solution.py:356
  32.1 10.0 %collective-permute-start.12 = (bf16[144,512]{1,0:T(8,128)(2,1)}, bf16[144,512]{1,0:T(8,128)(2,1)}, u32[]{:S(2)}, u32[]{:S(2)}) collective-permute-start(bf16[144,512]{1,0:T(8,128)(2,1)} %collective-permute-done.5.refs_6_), channel_id=1, source_target_pairs={{8,9},{9,8},{11,10},{12,13},{13,12},{15,14},{24,25},{25,24},{27,26... | collective-permute-start | bytes 442376 | tf_op jit(solution)/shard_map/ppermute | solution.py:356
  35.8 6.4 %collective-permute-start.11 = (bf16[144,512]{1,0:T(8,128)(2,1)}, bf16[144,512]{1,0:T(8,128)(2,1)}, u32[]{:S(2)}, u32[]{:S(2)}) collective-permute-start(bf16[144,512]{1,0:T(8,128)(2,1)} %collective-permute-done.4.refs_5_), channel_id=1, source_target_pairs={{4,5},{5,4},{6,7},{7,6},{8,9},{9,8},{10,11},{11,10},{12,13},{13,12... | collective-permute-start | bytes 442376 | tf_op jit(solution)/shard_map/ppermute | solution.py:356
  37.7 1.2 %copy-start.3 = (bf16[128,4096]{1,0:T(8,128)(2,1)S(1)}, bf16[128,4096]{1,0:T(8,128)(2,1)}, u32[]{:S(2)}) copy-start(bf16[128,4096]{1,0:T(8,128)(2,1)} %q_ref.9) | copy-start | bytes 3145732
  39.0 1.2 %copy-start.5 = (bf16[128,4096]{1,0:T(8,128)(2,1)S(1)}, bf16[128,4096]{1,0:T(8,128)(2,1)}, u32[]{:S(2)}) copy-start(bf16[128,4096]{1,0:T(8,128)(2,1)} %x_ref.9) | copy-start | bytes 3145732
  42.2 0.9 copy-start.8
  43.1 0.9 copy-start.10
  44.0 0.9 copy-start.12
  45.6 35.1 %copy-start.4 = (bf16[128,4096]{1,0:T(8,128)(2,1)S(1)}, bf16[128,4096]{1,0:T(8,128)(2,1)}, u32[]{:S(2)}) copy-start(bf16[128,4096]{1,0:T(8,128)(2,1)} %q_ref.9) | copy-start | bytes 3145732
  45.6 35.1 %copy-start.6 = (bf16[128,4096]{1,0:T(8,128)(2,1)S(1)}, bf16[128,4096]{1,0:T(8,128)(2,1)}, u32[]{:S(2)}) copy-start(bf16[128,4096]{1,0:T(8,128)(2,1)} %x_ref.9) | copy-start | bytes 3145732
  57.3 5.7 %collective-permute-start.14 = (bf16[8,4096]{1,0:T(8,128)(2,1)S(1)}, bf16[8,4096]{1,0:T(8,128)(2,1)S(1)}, u32[]{:S(2)}, u32[]{:S(2)}) collective-permute-start(bf16[8,4096]{1,0:T(8,128)(2,1)S(1)} %get-tuple-element.20), channel_id=1, source_target_pairs={{0,4},{1,5},{2,6},{3,7},{4,8},{5,9},{6,10},{7,11},{8,12},{9,13},{1... | collective-permute-start | bytes 196616 | tf_op jit(solution)/shard_map/ppermute | solution.py:356
  57.4 8.3 %collective-permute-start.15 = (bf16[8,4096]{1,0:T(8,128)(2,1)S(1)}, bf16[8,4096]{1,0:T(8,128)(2,1)S(1)}, u32[]{:S(2)}, u32[]{:S(2)}) collective-permute-start(bf16[8,4096]{1,0:T(8,128)(2,1)S(1)} %get-tuple-element.21), channel_id=1, source_target_pairs={{0,8},{1,9},{2,10},{3,11},{4,12},{5,13},{6,14},{7,15},{8,0},{9,1},... | collective-permute-start | bytes 196616 | tf_op jit(solution)/shard_map/ppermute | solution.py:356
  57.5 8.2 %collective-permute-start.16 = (bf16[8,4096]{1,0:T(8,128)(2,1)S(1)}, bf16[8,4096]{1,0:T(8,128)(2,1)S(1)}, u32[]{:S(2)}, u32[]{:S(2)}) collective-permute-start(bf16[8,4096]{1,0:T(8,128)(2,1)S(1)} %get-tuple-element.22), channel_id=1, source_target_pairs={{0,12},{1,13},{2,14},{3,15},{4,0},{5,1},{6,2},{7,3},{8,4},{9,5},{1... | collective-permute-start | bytes 196616 | tf_op jit(solution)/shard_map/ppermute | solution.py:356
  59.4 6.3 %collective-permute-start.21 = (bf16[8,4096]{1,0:T(8,128)(2,1)S(1)}, bf16[8,4096]{1,0:T(8,128)(2,1)S(1)}, u32[]{:S(2)}, u32[]{:S(2)}) collective-permute-start(bf16[8,4096]{1,0:T(8,128)(2,1)S(1)} %get-tuple-element.19._.refs_0_), channel_id=1, source_target_pairs={{0,1},{1,0},{2,3},{3,2},{4,5},{5,4},{6,7},{7,6},{8,9},{9,8},{10,11... | collective-permute-start | bytes 196616 | tf_op jit(solution)/shard_map/ppermute | solution.py:356
  59.4 8.4 %collective-permute-start.17 = (bf16[8,4096]{1,0:T(8,128)(2,1)S(1)}, bf16[8,4096]{1,0:T(8,128)(2,1)S(1)}, u32[]{:S(2)}, u32[]{:S(2)}) collective-permute-start(bf16[8,4096]{1,0:T(8,128)(2,1)S(1)} %get-tuple-element.19._.refs_0_), channel_id=1, source_target_pairs={{0,2},{1,3},{2,0},{3,1},{4,6},{5,7},{6,4},{7,5},{8,10},{9,11},{10,... | collective-permute-start | bytes 196616 | tf_op jit(solution)/shard_map/ppermute | solution.py:356
  63.0 4.9 %collective-permute-start.22 = (bf16[8,4096]{1,0:T(8,128)(2,1)S(1)}, bf16[8,4096]{1,0:T(8,128)(2,1)S(1)}, u32[]{:S(2)}, u32[]{:S(2)}) collective-permute-start(bf16[8,4096]{1,0:T(8,128)(2,1)S(1)} %collective-permute-done.14.refs_1_), channel_id=1, source_target_pairs={{0,1},{1,0},{2,3},{3,2},{4,5},{5,4},{6,7},{7,6},{8,9},{9,8},{10,11... | collective-permute-start | bytes 196616 | tf_op jit(solution)/shard_map/ppermute | solution.py:356
  65.7 4.8 %collective-permute-start.18 = (bf16[8,4096]{1,0:T(8,128)(2,1)S(1)}, bf16[8,4096]{1,0:T(8,128)(2,1)S(1)}, u32[]{:S(2)}, u32[]{:S(2)}) collective-permute-start(bf16[8,4096]{1,0:T(8,128)(2,1)S(1)} %collective-permute-done.14.refs_1_), channel_id=1, source_target_pairs={{0,2},{1,3},{2,0},{3,1},{4,6},{5,7},{6,4},{7,5},{8,10},{9,11},{10,... | collective-permute-start | bytes 196616 | tf_op jit(solution)/shard_map/ppermute | solution.py:356
  65.7 4.8 %collective-permute-start.23 = (bf16[8,4096]{1,0:T(8,128)(2,1)S(1)}, bf16[8,4096]{1,0:T(8,128)(2,1)S(1)}, u32[]{:S(2)}, u32[]{:S(2)}) collective-permute-start(bf16[8,4096]{1,0:T(8,128)(2,1)S(1)} %collective-permute-done.15.refs_2_), channel_id=1, source_target_pairs={{0,1},{1,0},{2,3},{3,2},{4,5},{5,4},{6,7},{7,6},{8,9},{9,8},{10,11... | collective-permute-start | bytes 196616 | tf_op jit(solution)/shard_map/ppermute | solution.py:356
  65.7 6.1 %collective-permute-start.19 = (bf16[8,4096]{1,0:T(8,128)(2,1)S(1)}, bf16[8,4096]{1,0:T(8,128)(2,1)S(1)}, u32[]{:S(2)}, u32[]{:S(2)}) collective-permute-start(bf16[8,4096]{1,0:T(8,128)(2,1)S(1)} %collective-permute-done.15.refs_2_), channel_id=1, source_target_pairs={{0,2},{1,3},{2,0},{3,1},{4,6},{5,7},{6,4},{7,5},{8,10},{9,11},{10,... | collective-permute-start | bytes 196616 | tf_op jit(solution)/shard_map/ppermute | solution.py:356
  67.8 4.8 %collective-permute-start.20 = (bf16[8,4096]{1,0:T(8,128)(2,1)S(1)}, bf16[8,4096]{1,0:T(8,128)(2,1)S(1)}, u32[]{:S(2)}, u32[]{:S(2)}) collective-permute-start(bf16[8,4096]{1,0:T(8,128)(2,1)S(1)} %collective-permute-done.16.refs_3_), channel_id=1, source_target_pairs={{0,2},{1,3},{2,0},{3,1},{4,6},{5,7},{6,4},{7,5},{8,10},{9,11},{10,... | collective-permute-start | bytes 196616 | tf_op jit(solution)/shard_map/ppermute | solution.py:356
  67.9 4.7 %collective-permute-start.24 = (bf16[8,4096]{1,0:T(8,128)(2,1)S(1)}, bf16[8,4096]{1,0:T(8,128)(2,1)S(1)}, u32[]{:S(2)}, u32[]{:S(2)}) collective-permute-start(bf16[8,4096]{1,0:T(8,128)(2,1)S(1)} %collective-permute-done.16.refs_3_), channel_id=1, source_target_pairs={{0,1},{1,0},{2,3},{3,2},{4,5},{5,4},{6,7},{7,6},{8,9},{9,8},{10,11... | collective-permute-start | bytes 196616 | tf_op jit(solution)/shard_map/ppermute | solution.py:356
  70.5 2.1 %collective-permute-start.25 = (bf16[8,4096]{1,0:T(8,128)(2,1)S(1)}, bf16[8,4096]{1,0:T(8,128)(2,1)S(1)}, u32[]{:S(2)}, u32[]{:S(2)}) collective-permute-start(bf16[8,4096]{1,0:T(8,128)(2,1)S(1)} %collective-permute-done.17.refs_4_), channel_id=1, source_target_pairs={{0,1},{1,0},{2,3},{3,2},{4,5},{5,4},{6,7},{7,6},{8,9},{9,8},{10,11... | collective-permute-start | bytes 196616 | tf_op jit(solution)/shard_map/ppermute | solution.py:356
  70.5 2.1 %collective-permute-start.26 = (bf16[8,4096]{1,0:T(8,128)(2,1)S(1)}, bf16[8,4096]{1,0:T(8,128)(2,1)S(1)}, u32[]{:S(2)}, u32[]{:S(2)}) collective-permute-start(bf16[8,4096]{1,0:T(8,128)(2,1)S(1)} %collective-permute-done.18.refs_5_), channel_id=1, source_target_pairs={{0,1},{1,0},{2,3},{3,2},{4,5},{5,4},{6,7},{7,6},{8,9},{9,8},{10,11... | collective-permute-start | bytes 196616 | tf_op jit(solution)/shard_map/ppermute | solution.py:356
  71.8 1.3 %collective-permute-start.27 = (bf16[8,4096]{1,0:T(8,128)(2,1)S(1)}, bf16[8,4096]{1,0:T(8,128)(2,1)S(1)}, u32[]{:S(2)}, u32[]{:S(2)}) collective-permute-start(bf16[8,4096]{1,0:T(8,128)(2,1)S(1)} %collective-permute-done.19.refs_6_), channel_id=1, source_target_pairs={{0,1},{1,0},{2,3},{3,2},{4,5},{5,4},{6,7},{7,6},{8,9},{9,8},{10,11... | collective-permute-start | bytes 196616 | tf_op jit(solution)/shard_map/ppermute | solution.py:356
  72.6 1.3 %collective-permute-start.28 = (bf16[8,4096]{1,0:T(8,128)(2,1)S(1)}, bf16[8,4096]{1,0:T(8,128)(2,1)S(1)}, u32[]{:S(2)}, u32[]{:S(2)}) collective-permute-start(bf16[8,4096]{1,0:T(8,128)(2,1)S(1)} %collective-permute-done.20.refs_7_), channel_id=1, source_target_pairs={{0,1},{1,0},{2,3},{3,2},{4,5},{5,4},{6,7},{7,6},{8,9},{9,8},{10,11... | collective-permute-start | bytes 196616 | tf_op jit(solution)/shard_map/ppermute | solution.py:356
  73.8 1.9 %copy-start.1 = (bf16[1,4096,384]{2,1,0:T(8,128)(2,1)S(1)}, bf16[1,4096,384]{2,1,0:T(8,128)(2,1)}, u32[]{:S(2)}) copy-start(bf16[1,4096,384]{2,1,0:T(8,128)(2,1)} %refs_17_.1) | copy-start | bytes 9437188
  75.7 1.9 %copy-start.2 = (bf16[1,384,4096]{2,1,0:T(8,128)(2,1)S(1)}, bf16[1,384,4096]{2,1,0:T(8,128)(2,1)}, u32[]{:S(2)}) copy-start(bf16[1,384,4096]{2,1,0:T(8,128)(2,1)} %refs_18_.1) | copy-start | bytes 9437188
  80.5 8.5 %collective-permute-start.29 = (bf16[64,4096]{1,0:T(8,128)(2,1)S(1)}, bf16[64,4096]{1,0:T(8,128)(2,1)S(1)}, u32[]{:S(2)}, u32[]{:S(2)}) collective-permute-start(bf16[64,4096]{1,0:T(8,128)(2,1)S(1)} %get-tuple-element.24), channel_id=1, source_target_pairs={{0,1},{1,0},{2,3},{3,2},{4,5},{5,4},{6,7},{7,6},{8,9},{9,8},{10,11... | collective-permute-start | bytes 1572872 | tf_op jit(solution)/shard_map/ppermute | solution.py:356
  89.1 16.8 %collective-permute-start.30 = (bf16[32,4096]{1,0:T(8,128)(2,1)S(1)}, bf16[32,4096]{1,0:T(8,128)(2,1)S(1)}, u32[]{:S(2)}, u32[]{:S(2)}) collective-permute-start(bf16[32,4096]{1,0:T(8,128)(2,1)S(1)} %slice.35), channel_id=1, source_target_pairs={{0,2},{1,3},{2,0},{3,1},{4,6},{5,7},{6,4},{7,5},{8,10},{9,11},{10,... | collective-permute-start | bytes 786440 | tf_op jit(solution)/shard_map/ppermute | solution.py:356
  106.0 10.3 %collective-permute-start.33 = (bf16[8,4096]{1,0:T(8,128)(2,1)S(1)}, bf16[8,4096]{1,0:T(8,128)(2,1)S(1)}, u32[]{:S(2)}, u32[]{:S(2)}) collective-permute-start(bf16[8,4096]{1,0:T(8,128)(2,1)S(1)} %get-tuple-element.25), channel_id=1, source_target_pairs={{0,4},{1,5},{2,6},{3,7},{4,8},{5,9},{6,10},{7,11},{8,12},{9,13},{1... | collective-permute-start | bytes 196616 | tf_op jit(solution)/shard_map/ppermute | solution.py:356
  106.0 10.3 %collective-permute-start.32 = (bf16[8,4096]{1,0:T(8,128)(2,1)S(1)}, bf16[8,4096]{1,0:T(8,128)(2,1)S(1)}, u32[]{:S(2)}, u32[]{:S(2)}) collective-permute-start(bf16[8,4096]{1,0:T(8,128)(2,1)S(1)} %get-tuple-element.26), channel_id=1, source_target_pairs={{0,8},{1,9},{2,10},{3,11},{4,12},{5,13},{6,14},{7,15},{8,0},{9,1},... | collective-permute-start | bytes 196616 | tf_op jit(solution)/shard_map/ppermute | solution.py:356
  106.1 10.2 %copy-start.17 = (s32[128,4]{0,1:T(4,128)S(1)}, s32[128,4]{0,1:T(4,128)}, u32[]{:S(2)}) copy-start(s32[128,4]{0,1:T(4,128)} %param.17) | copy-start | bytes 6148
  106.1 10.2 %copy-start.20 = (f32[128,4]{0,1:T(4,128)S(1)}, f32[128,4]{0,1:T(4,128)}, u32[]{:S(2)}) copy-start(f32[128,4]{0,1:T(4,128)} %param.18) | copy-start | bytes 6148
  106.1 10.2 %collective-permute-start.31 = (bf16[8,4096]{1,0:T(8,128)(2,1)S(1)}, bf16[8,4096]{1,0:T(8,128)(2,1)S(1)}, u32[]{:S(2)}, u32[]{:S(2)}) collective-permute-start(bf16[8,4096]{1,0:T(8,128)(2,1)S(1)} %get-tuple-element.27), channel_id=1, source_target_pairs={{0,12},{1,13},{2,14},{3,15},{4,0},{5,1},{6,2},{7,3},{8,4},{9,5},{1... | collective-permute-start | bytes 196616 | tf_op jit(solution)/shard_map/ppermute | solution.py:356
  (7 other events, 4.7 us)

commit v2 on v1

--- a/solution.py
+++ b/solution.py
@@ -96,17 +96,14 @@
             [known[0:1], known[1:2] + (1.0 - known[2:3]) * docs[:, 0:1], known[2:]], axis=0
         )
         for h in range(KV_HEADS):
-            for g in range(0, GROUP, 2):
-                a = h * GROUP + g
-                two = jnp.concatenate(
-                    [
-                        q_rows[k * SLOTS : (k + 1) * SLOTS, i * HEAD : (i + 1) * HEAD]
-                        for i in (a, a + 1)
-                    ],
-                    axis=0,
-                )
-                at = k * TILE + g * SLOTS
-                qs_ref[h, at : at + 2 * SLOTS, :] = two.astype(BF16)
+            stack = jnp.concatenate(
+                [
+                    q_rows[k * SLOTS : (k + 1) * SLOTS, a * HEAD : (a + 1) * HEAD]
+                    for a in range(h * GROUP, (h + 1) * GROUP)
+                ],
+                axis=0,
+            )
+            qs_ref[h, :, k * TILE : (k + 1) * TILE] = stack.T.astype(BF16)
 
 
 def doc_starts(n, pos, held):
@@ -157,7 +154,7 @@
                 ],
                 axis=1,
             )
-            scores = dot(keys, queries[i](), 1, 1)
+            scores = dot(keys, queries[i]())
             if masked:
                 scores = scores + bias_ref[...]
             new_top = jnp.maximum(top, jnp.max(scores, axis=0, keepdims=True))
@@ -184,7 +181,8 @@
     pos = pos_ref[0]
     z, y, c = pos // SHARDS, (pos // 2) % 2, pos % 2
     copies = []
-    for i, (flip_c, flip_y, k) in enumerate(senders):
+    for i, (flip_c, *ways) in enumerate(senders):
+        flip_y, k = (jnp.where(y == 0, ways[0][j], ways[1][j]) for j in range(2))
         sender = lax.rem(z - k + planes, planes) * SHARDS + (y ^ flip_y) * 2 + (c ^ flip_c)
         copies.append(pltpu.make_async_copy(pieces[i], held.at[sender], sems.at[i]))
     for copy in copies:
@@ -201,7 +199,7 @@
         done = flash(
             pos,
             held,
-            [lambda h=h, at=at: qs_ref[h, at : at + lanes, :] for h in range(KV_HEADS)],
+            [lambda h=h, at=at: qs_ref[h, :, at : at + lanes] for h in range(KV_HEADS)],
             list(range(KV_HEADS)),
             acc,
             bias,
@@ -225,15 +223,8 @@
 
 def expert_kernel(count, *refs):
     pieces = refs[:count]
-    weights = refs[count : count + 3]
-    keep_ref, send_ref = refs[count + 3 : count + 5]
-    wg, wu, wd, rows, sems = refs[count + 5 :]
-    loads = [
-        pltpu.make_async_copy(src.at[0], dst, sems.at[i])
-        for i, (src, dst) in enumerate(zip(weights, (wg, wu, wd)))
-    ]
-    for load in loads:
-        load.start()
+    wg, wu, wd = refs[count : count + 3]
+    keep_ref, send_ref, rows = refs[count + 4 :]
     width = rows.shape[1]
     batch = min(count, 16)
     step = 1024
@@ -244,15 +235,9 @@
                     [pieces[b * batch + i + t][:, col : col + step].astype(F32) for t in range(2)],
                     axis=0,
                 ).astype(BF16)
-        if b == 0:
-            loads[0].wait()
         gate = dot(rows[...], wg[...])
-        if b == 0:
-            loads[1].wait()
         up = dot(rows[...], wu[...])
         act = (gate / (1.0 + jnp.exp(-gate)) * up).astype(BF16)
-        if b == 0:
-            loads[2].wait()
         out_rows = batch * SLOTS
         for col in range(0, width, step):
             part = dot(act, wd[:, col : col + step]).astype(BF16)
@@ -267,7 +252,17 @@
                 send_ref[at - half : at - half + out_rows, col : col + step] = part
 
 
-def own_kernel(n, part, pos_ref, held, q_ref, x_ref, _, h_ref, acc, bias):
+def own_kernel(n, part, loads, pos_ref, held, q_ref, x_ref, _, *refs):
+    sources, (h_ref, done_ref) = refs[:loads], refs[loads : loads + 2]
+    targets = refs[loads + 2 : 2 * loads + 2]
+    acc, bias, qt, sems = refs[2 * loads + 2 :]
+    moves = [
+        pltpu.make_async_copy(source.at[0], target, sems.at[i])
+        for i, (source, target) in enumerate(zip(sources, targets))
+    ]
+    for move in moves:
+        move.start()
+    done_ref[...] = jnp.zeros((8, TILE), F32)
     pos = pos_ref[0]
     starts = doc_starts(n, pos, held)
     first = starts_of(held[pos, TILE:KV_ROWS, 0:HEAD].astype(F32)[0:1], starts)
@@ -275,15 +270,14 @@
     place = jnp.concatenate([place] * 2, axis=1)
     first = jnp.concatenate([first] * 2, axis=1)
 
-    def rows(i):
-        return jnp.concatenate(
-            [q_ref[:, a * HEAD : (a + 1) * HEAD] for a in (2 * i, 2 * i + 1)], axis=0
-        )
-
+    for a in range(8):
+        qt[a // 2, :, (a % 2) * TILE : (a % 2 + 1) * TILE] = (
+            q_ref[:, a * HEAD : (a + 1) * HEAD].astype(F32).T.astype(BF16)
+        )
     done = flash(
         pos,
         held,
-        [lambda i=i: rows(i) for i in range(4)],
+        [lambda i=i: qt[i] for i in range(4)],
         [part // 2] * 4,
         acc,
         bias,
@@ -296,6 +290,8 @@
             h_ref[:, lane : lane + HEAD] = (
                 x_ref[:, lane : lane + HEAD].astype(F32) + done[i][g * TILE : (g + 1) * TILE]
             )
+    for move in moves:
+        move.wait()
 
 
 def combine_kernel(planes, pos_ref, routes_ref, gates_ref, *refs):
@@ -348,46 +344,45 @@
             pltpu.VMEM((tokens, KV_HEADS * HEAD), BF16),
             pltpu.SemaphoreType.DMA((3,)),
         ],
-        compiler_params=params(small),
+        compiler_params=params(60),
         name="pack",
     )(docs, keys, values)
 
     def move(value, pairs):
         return lax.ppermute(value, "expert", pairs)
 
-    def needed(tile, devices):
-        return any(tile <= t <= tile + back for t in devices)
-
-    kv = {(0, 0, 0): packed}
-    for k in range(1, planes):
-        pairs = [
-            (s, s + k * SHARDS)
-            for s in range(n - k * SHARDS)
-            if needed(s, [(s // SHARDS + k) * SHARDS + j for j in range(SHARDS)])
+    def needed(k, y_from, y_to):
+        gaps = [
+            k * SHARDS + 2 * (y_to - y_from) + (to - of) for to in range(2) for of in range(2)
         ]
-        if pairs:
-            kv[0, 0, k] = move(packed, pairs)
-    for (_, _, k), piece in list(kv.items()):
-        pairs = [
-            (d, d ^ 2)
-            for d in range(n)
-            if d >= k * SHARDS and needed(d - k * SHARDS, [d ^ 2, d ^ 3])
-        ]
-        if pairs:
-            kv[0, 1, k] = move(piece, pairs)
-    for (_, flip_y, k), piece in list(kv.items()):
-        pairs = [
-            (d, d ^ 1)
-            for d in range(n)
-            if d >= k * SHARDS and needed((d - k * SHARDS) ^ (2 * flip_y), [d ^ 1])
-        ]
-        if pairs:
-            kv[1, flip_y, k] = move(piece, pairs)
+        return any(0 <= gap <= back for gap in gaps)
+
+    far = max(k for k in range(planes) if any(needed(k, a, b) for a in (0, 1) for b in (0, 1)))
+    along = [packed]
+    for k in range(1, far + 1):
+        used = [any(needed(k, y, to) for to in (0, 1)) for y in (0, 1)]
+        along.append(
+            move(
+                packed,
+                [(s, (s + k * SHARDS) % n if used[s // 2 % 2] else s) for s in range(n)],
+            )
+        )
+    kv = {(0, (0, k), (0, k)): piece for k, piece in enumerate(along)}
+    flips = [(s, s ^ 2) for s in range(n)]
+    alone = far > 0 and not needed(0, 1, 0) and not needed(far, 0, 1)
+    for k in range(1 if alone else 0, far if alone else far + 1):
+        pairs = [(s, s ^ 2 if s >= k * SHARDS else s) for s in range(n)]
+        kv[0, (1, k), (1, k)] = move(along[k], pairs)
+    if alone:
+        odd = (pos[0] & 2) != 0
+        kv[0, (1, far), (1, 0)] = move(jnp.where(odd, along[far], packed), flips)
+    for (_, *ways), piece in list(kv.items()):
+        kv[1, ways[0], ways[1]] = move(piece, [(s, s ^ 1) for s in range(n)])
 
     q_rows, x_rows, facts = pl.pallas_call(
         functools.partial(select_kernel, planes),
         out_shape=[
-            jax.ShapeDtypeStruct((KV_HEADS, planes * TILE, HEAD), BF16),
+            jax.ShapeDtypeStruct((KV_HEADS, HEAD, planes * TILE), BF16),
             jax.ShapeDtypeStruct((planes * SLOTS, width), F32),
             jax.ShapeDtypeStruct((8, planes * TILE), F32),
         ],
@@ -413,26 +408,38 @@
         name="routed",
     )(pos, norm_gain.reshape(1, width), q_rows, x_rows, facts, *kv.values())
 
-    def own(part, after):
+    def own(part, after, *sources):
         columns = pl.BlockSpec((tokens, 8 * HEAD), lambda i: (0, part))
         return pl.pallas_call(
-            functools.partial(own_kernel, n, part),
-            out_shape=jax.ShapeDtypeStruct((tokens, 8 * HEAD), F32),
+            functools.partial(own_kernel, n, part, len(sources)),
+            out_shape=[
+                jax.ShapeDtypeStruct((tokens, 8 * HEAD), F32),
+                jax.ShapeDtypeStruct((8, TILE), F32),
+            ]
+            + [jax.ShapeDtypeStruct(w.shape[1:], BF16) for w in sources],
             grid=(1,),
-            in_specs=[SMEM, VMEM, columns, columns, ANY],
-            out_specs=pl.BlockSpec((tokens, 8 * HEAD), lambda i: (0, 0)),
+            in_specs=[SMEM, VMEM, columns, columns, ANY] + [HBM] * len(sources),
+            out_specs=[
+                pl.BlockSpec((tokens, 8 * HEAD), lambda i: (0, 0)),
+                pl.BlockSpec((8, TILE), lambda i: (0, 0)),
+            ]
+            + [VMEM] * len(sources),
             scratch_shapes=[
                 pltpu.VMEM((4, HEAD, 2 * TILE), F32),
                 pltpu.VMEM((KEYS, 2 * TILE), F32),
+                pltpu.VMEM((4, HEAD, 2 * TILE), BF16),
+                pltpu.SemaphoreType.DMA((3,)),
             ],
-            compiler_params=params(small),
+            compiler_params=params(39 if sources and n <= 16 else small),
             cost_estimate=pl.CostEstimate(
                 flops=2_000_000_000, bytes_accessed=8_000_000, transcendentals=2_000_000
             ),
             name="own",
-        )(pos, held, queries, resid, after)
-
-    halves = [own(part, sent[0]) for part in range(2)]
+        )(pos, held, queries, resid, after, *sources)
+
+    half0, done = own(0, sent[0])
+    half1, done, *weights = own(1, done, w_gate, w_up, w_down)
+    halves = [half0, half1]
 
     pieces = [sent[0]]
     for k in range(1, planes):
@@ -444,23 +451,17 @@
     keep, send = pl.pallas_call(
         functools.partial(expert_kernel, n),
         out_shape=[half, half],
-        in_specs=[VMEM] * n + [HBM] * 3,
+        in_specs=[VMEM] * (n + 3) + [ANY],
         out_specs=[VMEM, VMEM],
-        scratch_shapes=[
-            pltpu.VMEM((width, hidden), BF16),
-            pltpu.VMEM((width, hidden), BF16),
-            pltpu.VMEM((hidden, width), BF16),
-            pltpu.VMEM((16 * SLOTS, width), BF16),
-            pltpu.SemaphoreType.DMA((3,)),
-        ],
-        compiler_params=params(small),
+        scratch_shapes=[pltpu.VMEM((16 * SLOTS, width), BF16)],
+        compiler_params=params(16),
         cost_estimate=pl.CostEstimate(
             flops=1_200_000_000, bytes_accessed=12_000_000, transcendentals=50_000
         ),
         name="expert",
-    )(*pieces, w_gate, w_up, w_down)
-
-    halves += [own(part, keep) for part in range(2, 4)]
+    )(*pieces, *weights, done)
+
+    halves += [own(part, keep)[0] for part in range(2, 4)]
 
     total = keep.astype(F32) + move(send, [(s, s ^ 1) for s in range(n)]).astype(F32)
     quarter = n * SLOTS // 4

time: 118 us -> 99.8 us (0.85)
  local copies, waits for them, and re-layouts: 15.5 us -> 5.48 us
  starting transfers between devices: 35.5 us -> 29.4 us
  waiting for transfers between devices: 16.2 us -> 13 us
    unnamed x42 -> x20, local copies, waits for them, and re-layouts: 15.4 us -> 5.43 us
    ppermute x34 -> x33, starting transfers between devices: 35.5 us -> 29.4 us  [move(): return lax.ppermute(value, 'expert', pairs)]
    ppermute x34 -> x33, waiting for transfers between devices: 16.2 us -> 13 us  [move(): return lax.ppermute(value, 'expert', pairs)]
    pallas_call x1, Pallas kernels: 0.2 us -> 1.64 us  [local(): pl.pallas_call(pack_kernel, out_shape=jax.ShapeDtypeStruct((KV_ROWS, 4 *...]
  transfers between devices with their start and end apart: 34 -> 33, of which waited for: 8 -> 6; matrix products, arithmetic and copies ran while one was open for 0% -> 1% of each run, Pallas kernels for 29% -> 33%
where the time goes in v2:
time: 99.8 us; the launch traced here: 100 us
  Pallas kernels  50.9 us (51%)
  starting transfers between devices  29.4 us (29%)
  waiting for transfers between devices  13 us (13%)
  local copies, waits for them, and re-layouts  5.48 us (5%)
  other arithmetic  1.11 us (1%)
    pallas_call x4, Pallas kernels, own(): pl.pallas_call(functools.partial(own_kernel, n, part, len(sources)), out_...  32.6 us
    ppermute x33, starting transfers between devices, move(): return lax.ppermute(value, 'expert', pairs)  29.4 us
    ppermute x33, waiting for transfers between devices, move(): return lax.ppermute(value, 'expert', pairs)  13 us
    pallas_call x1, Pallas kernels, local(): pl.pallas_call(functools.partial(routed_kernel, n, list(kv)), out_shape=[...  12.3 us
    unnamed x20, local copies, waits for them, and re-layouts  5.43 us
  transfers between devices with their start and end apart: 33, of which 6 were waited for; matrix products, arithmetic and copies ran while one was open for 1% of the time, Pallas kernels for 33%

profile of v2, /device:TPU:26, one launch (start us, length us, event | category | flops | bytes accessed | tf_op | source)
XLA Modules:
  0.0 100.2 jit_solution(16050435748671808580)
XLA Ops:
  0.0 1.6 %pack.1.refs_0_ = bf16[144,512]{1,0:T(8,128)(2,1)} custom-call(s32[1,128]{1,0:T(1,128)} %bitcast.8, bf16[128,256]{1,0:T(8,128)(2,1)} %keys_ref.1, bf16[128,256]{1,0:T(8,128)(2,1)} %values_ref.1), custom_call_target="tpu_custom_call" | custom-call | tf_op jit(solution)/shard_map/pack/pallas_call | solution.py:337
  1.6 1.6 %collective-permute-start.2 = (bf16[144,512]{1,0:T(8,128)(2,1)}, bf16[144,512]{1,0:T(8,128)(2,1)S(1)}, u32[]{:S(2)}, u32[]{:S(2)}) collective-permute-start(bf16[144,512]{1,0:T(8,128)(2,1)} %pack.1.refs_0_), channel_id=1, source_target_pairs={{0,0},{1,1},{2,14},{3,15},{4,4},{5,5},{6,2},{7,3},{8,8},{9,9},{10,... | collective-permute-start | bytes 442376 | tf_op jit(solution)/shard_map/ppermute | solution.py:352
  3.2 0.3 collective-permute-start.1
  3.6 2.5 %collective-permute-start = (bf16[144,512]{1,0:T(8,128)(2,1)}, bf16[144,512]{1,0:T(8,128)(2,1)S(1)}, u32[]{:S(2)}, u32[]{:S(2)}) collective-permute-start(bf16[144,512]{1,0:T(8,128)(2,1)} %pack.1.refs_0_), channel_id=1, source_target_pairs={{0,4},{1,5},{2,6},{3,7},{4,8},{5,9},{6,10},{7,11},{8,12},{9,13},{1... | collective-permute-start | bytes 442376 | tf_op jit(solution)/shard_map/ppermute | solution.py:352
  6.0 1.0 broadcast_select_fusion
  7.0 7.0 %collective-permute-start.5 = (bf16[144,512]{1,0:T(8,128)(2,1)S(1)}, bf16[144,512]{1,0:T(8,128)(2,1)S(1)}, u32[]{:S(2)}, u32[]{:S(2)}) collective-permute-start(bf16[144,512]{1,0:T(8,128)(2,1)S(1)} %broadcast_select_fusion), channel_id=1, source_target_pairs={{0,2},{1,3},{2,0},{3,1},{4,6},{5,7},{6,4},{7,5},{8,10},{9,11},{10,... | collective-permute-start | bytes 442376 | tf_op jit(solution)/shard_map/ppermute | solution.py:352
  14.0 6.9 %collective-permute-start.4 = (bf16[144,512]{1,0:T(8,128)(2,1)S(1)}, bf16[144,512]{1,0:T(8,128)(2,1)S(1)}, u32[]{:S(2)}, u32[]{:S(2)}) collective-permute-start(bf16[144,512]{1,0:T(8,128)(2,1)S(1)} %collective-permute-done.1.refs_2_), channel_id=1, source_target_pairs={{0,0},{1,1},{2,2},{3,3},{4,4},{5,5},{6,6},{7,7},{8,10},{9,11},{10,... | collective-permute-start | bytes 442376 | tf_op jit(solution)/shard_map/ppermute | solution.py:352
  20.9 1.9 %collective-permute-start.3 = (bf16[144,512]{1,0:T(8,128)(2,1)S(1)}, bf16[144,512]{1,0:T(8,128)(2,1)S(1)}, u32[]{:S(2)}, u32[]{:S(2)}) collective-permute-start(bf16[144,512]{1,0:T(8,128)(2,1)S(1)} %collective-permute-done.refs_1_), channel_id=1, source_target_pairs={{0,0},{1,1},{2,2},{3,3},{4,6},{5,7},{6,4},{7,5},{8,10},{9,11},{10,... | collective-permute-start | bytes 442376 | tf_op jit(solution)/shard_map/ppermute | solution.py:352
  22.9 0.1 collective-permute-start.8
  23.0 0.5 collective-permute-start.7
  23.5 0.1 collective-permute-start.12
  23.5 1.6 %collective-permute-done.4.refs_5_ = bf16[144,512]{1,0:T(8,128)(2,1)S(1)} collective-permute-done((bf16[144,512]{1,0:T(8,128)(2,1)S(1)}, bf16[144,512]{1,0:T(8,128)(2,1)S(1)}, u32[]{:S(2)}, u32[]{:S(2)}) %collective-permute-start.4) | collective-permute-done | bytes 147488 | tf_op jit(solution)/shard_map/ppermute | solution.py:352
  25.1 3.2 %collective-permute-done.3.refs_4_ = bf16[144,512]{1,0:T(8,128)(2,1)S(1)} collective-permute-done((bf16[144,512]{1,0:T(8,128)(2,1)S(1)}, bf16[144,512]{1,0:T(8,128)(2,1)S(1)}, u32[]{:S(2)}, u32[]{:S(2)}) %collective-permute-start.3) | collective-permute-done | bytes 147488 | tf_op jit(solution)/shard_map/ppermute | solution.py:352
  28.3 1.2 %copy-done = bf16[128,4096]{1,0:T(8,128)(2,1)S(1)} copy-done((bf16[128,4096]{1,0:T(8,128)(2,1)S(1)}, bf16[128,4096]{1,0:T(8,128)(2,1)}, u32[]{:S(2)}) %copy-start) | copy-done | bytes 1048600
  29.6 1.2 %copy-done.2 = bf16[128,4096]{1,0:T(8,128)(2,1)S(1)} copy-done((bf16[128,4096]{1,0:T(8,128)(2,1)S(1)}, bf16[128,4096]{1,0:T(8,128)(2,1)}, u32[]{:S(2)}) %copy-start.2) | copy-done | bytes 1048600
  30.8 0.7 copy-done.6
  31.5 0.7 copy-done.8
  32.1 0.6 select.1
  32.8 0.9 copy-done.4
  33.7 0.7 copy-done.5
  34.4 12.3 %routed.1 = (bf16[8,4096]{1,0:T(8,128)(2,1)S(1)}, bf16[8,4096]{1,0:T(8,128)(2,1)S(1)}, bf16[8,4096]{1,0:T(8,128)(2,1)S(1)}, bf16[8,4096]{1,0:T(8,128)(2,1)S(1)}, bf16[16,144,512]{2,1,0:T(8,128)(2,1)S(1)}) custom-call(s32[1]{0:T(128)} %bitcast.pos_ref, f32[1,4096]{1,0:T(1,128)S(1)} %bitcast.5, bf16[2,128,512]{2,1,0:T(8,128)(2,1)S(1)} %get-tuple-element.24.qs_ref, ...), custom_call_target="tpu_custom_call" | custom-call | tf_op jit(solution)/shard_map/routed/pallas_call | solution.py:395
  46.7 0.1 collective-permute-start.13
  46.7 0.1 collective-permute-start.14
  46.8 1.9 %collective-permute-start.15 = (bf16[8,4096]{1,0:T(8,128)(2,1)S(1)}, bf16[8,4096]{1,0:T(8,128)(2,1)S(1)}, u32[]{:S(2)}, u32[]{:S(2)}) collective-permute-start(bf16[8,4096]{1,0:T(8,128)(2,1)S(1)} %get-tuple-element.34), channel_id=1, source_target_pairs={{0,12},{1,13},{2,14},{3,15},{4,0},{5,1},{6,2},{7,3},{8,4},{9,5},{1... | collective-permute-start | bytes 196616 | tf_op jit(solution)/shard_map/ppermute | solution.py:352
  48.8 0.1 collective-permute-start.16
  48.8 3.5 %collective-permute-done.13.refs_1_ = bf16[8,4096]{1,0:T(8,128)(2,1)S(1)} collective-permute-done((bf16[8,4096]{1,0:T(8,128)(2,1)S(1)}, bf16[8,4096]{1,0:T(8,128)(2,1)S(1)}, u32[]{:S(2)}, u32[]{:S(2)}) %collective-permute-start.13) | collective-permute-done | bytes 65568 | tf_op jit(solution)/shard_map/ppermute | solution.py:352
  52.3 2.7 %collective-permute-done.14.refs_2_ = bf16[8,4096]{1,0:T(8,128)(2,1)S(1)} collective-permute-done((bf16[8,4096]{1,0:T(8,128)(2,1)S(1)}, bf16[8,4096]{1,0:T(8,128)(2,1)S(1)}, u32[]{:S(2)}, u32[]{:S(2)}) %collective-permute-start.14) | collective-permute-done | bytes 65568 | tf_op jit(solution)/shard_map/ppermute | solution.py:352
  55.0 0.5 collective-permute-start.17
  55.5 1.6 %collective-permute-start.18 = (bf16[8,4096]{1,0:T(8,128)(2,1)S(1)}, bf16[8,4096]{1,0:T(8,128)(2,1)S(1)}, u32[]{:S(2)}, u32[]{:S(2)}) collective-permute-start(bf16[8,4096]{1,0:T(8,128)(2,1)S(1)} %collective-permute-done.14.refs_2_), channel_id=1, source_target_pairs={{0,2},{1,3},{2,0},{3,1},{4,6},{5,7},{6,4},{7,5},{8,10},{9,11},{10,... | collective-permute-start | bytes 196616 | tf_op jit(solution)/shard_map/ppermute | solution.py:352
  57.1 0.5 collective-permute-start.19
  57.6 8.1 %own.4 = (f32[128,1024]{1,0:T(8,128)S(1)}, f32[8,128]{1,0:T(8,128)S(1)}) custom-call(s32[1]{0:T(128)} %bitcast.pos_ref, bf16[16,144,512]{2,1,0:T(8,128)(2,1)S(1)} %get-tuple-element.27.held, bf16[128,4096]{1,0:T(8,128)(2,1)S(1)} %copy-done.1, bf16[128,4096]{1,0:T(8,128)(2,1)S(1)} %copy-done.3, bf16[8,4096]{1,0:T(8,128)(2,1)S(1)} %get-tuple-element.28._.refs_0_), custom_call_target="tpu_custom_call" | custom-call | flops 2000000000 | bytes 8000000 | tf_op jit(solution)/shard_map/own/pallas_call | solution.py:413
  65.7 0.1 collective-permute-start.23
  65.8 0.5 collective-permute-start.24
  66.3 0.1 collective-permute-start.25
  66.4 0.4 collective-permute-start.26
  66.8 0.1 collective-permute-start.27
  66.9 8.3 %own.5 = (f32[128,1024]{1,0:T(8,128)S(1)}, f32[8,128]{1,0:T(8,128)S(1)}, bf16[4096,384]{1,0:T(8,128)(2,1)S(1)}, bf16[4096,384]{1,0:T(8,128)(2,1)S(1)}, bf16[384,4096]{1,0:T(8,128)(2,1)S(1)}) custom-call(s32[1]{0:T(128)} %bitcast.pos_ref, bf16[16,144,512]{2,1,0:T(8,128)(2,1)S(1)} %get-tuple-element.27.held, bf16[128,4096]{1,0:T(8,128)(2,1)S(1)} %copy-done.1, ...), custom_call_target="tpu_custom_call" | custom-call | flops 2000000000 | bytes 8000000 | tf_op jit(solution)/shard_map/own/pallas_call | solution.py:413
  75.3 1.9 %expert.1 = (bf16[64,4096]{1,0:T(8,128)(2,1)S(1)}, bf16[64,4096]{1,0:T(8,128)(2,1)S(1)}) custom-call(bf16[8,4096]{1,0:T(8,128)(2,1)S(1)} %get-tuple-element.28._.refs_0_, bf16[8,4096]{1,0:T(8,128)(2,1)S(1)} %collective-permute-done.13.refs_1_, bf16[8,4096]{1,0:T(8,128)(2,1)S(1)} %collective-permute-done.14.refs_2_, ...), custom_call_target="tpu_custom_call" | custom-call | flops 1200000000 | bytes 12000000 | tf_op jit(solution)/shard_map/expert/pallas_call | solution.py:451
  77.2 0.5 collective-permute-start.28
  77.7 1.5 %collective-permute-done.28 = bf16[64,4096]{1,0:T(8,128)(2,1)S(1)} collective-permute-done((bf16[64,4096]{1,0:T(8,128)(2,1)S(1)}, bf16[64,4096]{1,0:T(8,128)(2,1)S(1)}, u32[]{:S(2)}, u32[]{:S(2)}) %collective-permute-start.28) | collective-permute-done | bytes 524320 | tf_op jit(solution)/shard_map/ppermute | solution.py:352
  79.2 0.1 convert_add_fusion
  79.4 0.1 collective-permute-start.29
  79.4 8.1 %own.7 = (f32[128,1024]{1,0:T(8,128)S(1)}, f32[8,128]{1,0:T(8,128)}) custom-call(s32[1]{0:T(128)} %bitcast.pos_ref, bf16[16,144,512]{2,1,0:T(8,128)(2,1)S(1)} %get-tuple-element.27.held, bf16[128,4096]{1,0:T(8,128)(2,1)S(1)} %copy-done.1, bf16[128,4096]{1,0:T(8,128)(2,1)S(1)} %copy-done.3, bf16[64,4096]{1,0:T(8,128)(2,1)S(1)} %get-tuple-element.39._), custom_call_target="tpu_custom_call" | custom-call | flops 2000000000 | bytes 8000000 | tf_op jit(solution)/shard_map/own/pallas_call | solution.py:413
  87.6 0.4 collective-permute-done.29
  88.1 0.1 collective-permute-start.31
  88.3 1.9 %collective-permute-start.30 = (bf16[8,4096]{1,0:T(8,128)(2,1)S(1)}, bf16[8,4096]{1,0:T(8,128)(2,1)S(1)}, u32[]{:S(2)}, u32[]{:S(2)}) collective-permute-start(bf16[8,4096]{1,0:T(8,128)(2,1)S(1)} %get-tuple-element.45), channel_id=1, source_target_pairs={{0,12},{1,13},{2,14},{3,15},{4,0},{5,1},{6,2},{7,3},{8,4},{9,5},{1... | collective-permute-start | bytes 196616 | tf_op jit(solution)/shard_map/ppermute | solution.py:352
  90.2 8.1 %own.6 = (f32[128,1024]{1,0:T(8,128)S(1)}, f32[8,128]{1,0:T(8,128)}) custom-call(s32[1]{0:T(128)} %bitcast.pos_ref, bf16[16,144,512]{2,1,0:T(8,128)(2,1)S(1)} %get-tuple-element.27.held, bf16[128,4096]{1,0:T(8,128)(2,1)S(1)} %copy-done.1, bf16[128,4096]{1,0:T(8,128)(2,1)S(1)} %copy-done.3, bf16[64,4096]{1,0:T(8,128)(2,1)S(1)} %get-tuple-element.39._), custom_call_target="tpu_custom_call" | custom-call | flops 2000000000 | bytes 8000000 | tf_op jit(solution)/shard_map/own/pallas_call | solution.py:413
  98.3 1.9 %combine.1 = bf16[128,4096]{1,0:T(8,128)(2,1)} custom-call(s32[1]{0:T(128)} %bitcast.pos_ref, s32[4,128]{1,0:T(4,128)S(1)} %bitcast.7, f32[4,128]{1,0:T(4,128)S(1)} %bitcast.10, f32[128,1024]{1,0:T(8,128)S(1)} %get-tuple-element.29.refs_0_, f32[128,1024]{1,0:T(8,128)S(1)} %get-tuple-element.31.refs_1_, f32[128,1024]{1,0:T(8,128)S(1)} %get-tuple-element.40.refs_2_, ...), custom_call_target="tpu_custom_call" | custom-call | tf_op jit(solution)/shard_map/combine/pallas_call | solution.py:478
  (52 shorter events, 0.3 us)
Async XLA Ops:
  1.6 4.4 %collective-permute-start.2 = (bf16[144,512]{1,0:T(8,128)(2,1)}, bf16[144,512]{1,0:T(8,128)(2,1)S(1)}, u32[]{:S(2)}, u32[]{:S(2)}) collective-permute-start(bf16[144,512]{1,0:T(8,128)(2,1)} %pack.1.refs_0_), channel_id=1, source_target_pairs={{0,0},{1,1},{2,14},{3,15},{4,4},{5,5},{6,2},{7,3},{8,8},{9,9},{10,... | collective-permute-start | bytes 442376 | tf_op jit(solution)/shard_map/ppermute | solution.py:352
  3.2 19.6 %collective-permute-start.6 = (bf16[144,512]{1,0:T(8,128)(2,1)}, bf16[144,512]{1,0:T(8,128)(2,1)S(1)}, u32[]{:S(2)}, u32[]{:S(2)}) collective-permute-start(bf16[144,512]{1,0:T(8,128)(2,1)} %pack.1.refs_0_), channel_id=1, source_target_pairs={{0,1},{1,0},{2,3},{3,2},{4,5},{5,4},{6,7},{7,6},{8,9},{9,8},{10,11... | collective-permute-start | bytes 442376 | tf_op jit(solution)/shard_map/ppermute | solution.py:352
  3.2 10.8 %collective-permute-start.1 = (bf16[144,512]{1,0:T(8,128)(2,1)}, bf16[144,512]{1,0:T(8,128)(2,1)S(1)}, u32[]{:S(2)}, u32[]{:S(2)}) collective-permute-start(bf16[144,512]{1,0:T(8,128)(2,1)} %pack.1.refs_0_), channel_id=1, source_target_pairs={{0,8},{1,9},{2,10},{3,11},{4,12},{5,13},{6,14},{7,15},{8,0},{9,1},... | collective-permute-start | bytes 442376 | tf_op jit(solution)/shard_map/ppermute | solution.py:352
  3.6 17.4 %collective-permute-start = (bf16[144,512]{1,0:T(8,128)(2,1)}, bf16[144,512]{1,0:T(8,128)(2,1)S(1)}, u32[]{:S(2)}, u32[]{:S(2)}) collective-permute-start(bf16[144,512]{1,0:T(8,128)(2,1)} %pack.1.refs_0_), channel_id=1, source_target_pairs={{0,4},{1,5},{2,6},{3,7},{4,8},{5,9},{6,10},{7,11},{8,12},{9,13},{1... | collective-permute-start | bytes 442376 | tf_op jit(solution)/shard_map/ppermute | solution.py:352
  7.0 16.0 %collective-permute-start.5 = (bf16[144,512]{1,0:T(8,128)(2,1)S(1)}, bf16[144,512]{1,0:T(8,128)(2,1)S(1)}, u32[]{:S(2)}, u32[]{:S(2)}) collective-permute-start(bf16[144,512]{1,0:T(8,128)(2,1)S(1)} %broadcast_select_fusion), channel_id=1, source_target_pairs={{0,2},{1,3},{2,0},{3,1},{4,6},{5,7},{6,4},{7,5},{8,10},{9,11},{10,... | collective-permute-start | bytes 442376 | tf_op jit(solution)/shard_map/ppermute | solution.py:352
  14.0 9.5 %collective-permute-start.9 = (bf16[144,512]{1,0:T(8,128)(2,1)S(1)}, bf16[144,512]{1,0:T(8,128)(2,1)S(1)}, u32[]{:S(2)}, u32[]{:S(2)}) collective-permute-start(bf16[144,512]{1,0:T(8,128)(2,1)S(1)} %collective-permute-done.2.refs_3_), channel_id=1, source_target_pairs={{0,1},{1,0},{2,3},{3,2},{4,5},{5,4},{6,7},{7,6},{8,9},{9,8},{10,11... | collective-permute-start | bytes 442376 | tf_op jit(solution)/shard_map/ppermute | solution.py:352
  14.0 11.1 %collective-permute-start.4 = (bf16[144,512]{1,0:T(8,128)(2,1)S(1)}, bf16[144,512]{1,0:T(8,128)(2,1)S(1)}, u32[]{:S(2)}, u32[]{:S(2)}) collective-permute-start(bf16[144,512]{1,0:T(8,128)(2,1)S(1)} %collective-permute-done.1.refs_2_), channel_id=1, source_target_pairs={{0,0},{1,1},{2,2},{3,3},{4,4},{5,5},{6,6},{7,7},{8,10},{9,11},{10,... | collective-permute-start | bytes 442376 | tf_op jit(solution)/shard_map/ppermute | solution.py:352
  20.9 7.4 %collective-permute-start.3 = (bf16[144,512]{1,0:T(8,128)(2,1)S(1)}, bf16[144,512]{1,0:T(8,128)(2,1)S(1)}, u32[]{:S(2)}, u32[]{:S(2)}) collective-permute-start(bf16[144,512]{1,0:T(8,128)(2,1)S(1)} %collective-permute-done.refs_1_), channel_id=1, source_target_pairs={{0,0},{1,1},{2,2},{3,3},{4,6},{5,7},{6,4},{7,5},{8,10},{9,11},{10,... | collective-permute-start | bytes 442376 | tf_op jit(solution)/shard_map/ppermute | solution.py:352
  22.9 9.9 %collective-permute-start.8 = (bf16[144,512]{1,0:T(8,128)(2,1)S(1)}, bf16[144,512]{1,0:T(8,128)(2,1)S(1)}, u32[]{:S(2)}, u32[]{:S(2)}) collective-permute-start(bf16[144,512]{1,0:T(8,128)(2,1)S(1)} %collective-permute-done.1.refs_2_), channel_id=1, source_target_pairs={{0,1},{1,0},{2,3},{3,2},{4,5},{5,4},{6,7},{7,6},{8,9},{9,8},{10,11... | collective-permute-start | bytes 442376 | tf_op jit(solution)/shard_map/ppermute | solution.py:352
  23.0 9.8 %collective-permute-start.7 = (bf16[144,512]{1,0:T(8,128)(2,1)S(1)}, bf16[144,512]{1,0:T(8,128)(2,1)S(1)}, u32[]{:S(2)}, u32[]{:S(2)}) collective-permute-start(bf16[144,512]{1,0:T(8,128)(2,1)S(1)} %collective-permute-done.refs_1_), channel_id=1, source_target_pairs={{0,1},{1,0},{2,3},{3,2},{4,5},{5,4},{6,7},{7,6},{8,9},{9,8},{10,11... | collective-permute-start | bytes 442376 | tf_op jit(solution)/shard_map/ppermute | solution.py:352
  23.5 9.3 %collective-permute-start.12 = (bf16[144,512]{1,0:T(8,128)(2,1)S(1)}, bf16[144,512]{1,0:T(8,128)(2,1)S(1)}, u32[]{:S(2)}, u32[]{:S(2)}) collective-permute-start(bf16[144,512]{1,0:T(8,128)(2,1)S(1)} %collective-permute-done.5.refs_6_), channel_id=1, source_target_pairs={{0,1},{1,0},{2,3},{3,2},{4,5},{5,4},{6,7},{7,6},{8,9},{9,8},{10,11... | collective-permute-start | bytes 442376 | tf_op jit(solution)/shard_map/ppermute | solution.py:352
  25.1 7.6 %collective-permute-start.11 = (bf16[144,512]{1,0:T(8,128)(2,1)S(1)}, bf16[144,512]{1,0:T(8,128)(2,1)S(1)}, u32[]{:S(2)}, u32[]{:S(2)}) collective-permute-start(bf16[144,512]{1,0:T(8,128)(2,1)S(1)} %collective-permute-done.4.refs_5_), channel_id=1, source_target_pairs={{0,1},{1,0},{2,3},{3,2},{4,5},{5,4},{6,7},{7,6},{8,9},{9,8},{10,11... | collective-permute-start | bytes 442376 | tf_op jit(solution)/shard_map/ppermute | solution.py:352
  28.3 4.4 %collective-permute-start.10 = (bf16[144,512]{1,0:T(8,128)(2,1)S(1)}, bf16[144,512]{1,0:T(8,128)(2,1)S(1)}, u32[]{:S(2)}, u32[]{:S(2)}) collective-permute-start(bf16[144,512]{1,0:T(8,128)(2,1)S(1)} %collective-permute-done.3.refs_4_), channel_id=1, source_target_pairs={{0,1},{1,0},{2,3},{3,2},{4,5},{5,4},{6,7},{7,6},{8,9},{9,8},{10,11... | collective-permute-start | bytes 442376 | tf_op jit(solution)/shard_map/ppermute | solution.py:352
  28.3 1.2 %copy-start = (bf16[128,4096]{1,0:T(8,128)(2,1)S(1)}, bf16[128,4096]{1,0:T(8,128)(2,1)}, u32[]{:S(2)}) copy-start(bf16[128,4096]{1,0:T(8,128)(2,1)} %q_ref.9) | copy-start | bytes 3145732
  29.6 1.2 %copy-start.2 = (bf16[128,4096]{1,0:T(8,128)(2,1)S(1)}, bf16[128,4096]{1,0:T(8,128)(2,1)}, u32[]{:S(2)}) copy-start(bf16[128,4096]{1,0:T(8,128)(2,1)} %x_ref.9) | copy-start | bytes 3145732
  30.8 0.7 copy-start.6
  31.5 0.7 copy-start.8
  32.1 25.5 %copy-start.1 = (bf16[128,4096]{1,0:T(8,128)(2,1)S(1)}, bf16[128,4096]{1,0:T(8,128)(2,1)}, u32[]{:S(2)}) copy-start(bf16[128,4096]{1,0:T(8,128)(2,1)} %q_ref.9) | copy-start | bytes 3145732
  32.1 25.5 %copy-start.3 = (bf16[128,4096]{1,0:T(8,128)(2,1)S(1)}, bf16[128,4096]{1,0:T(8,128)(2,1)}, u32[]{:S(2)}) copy-start(bf16[128,4096]{1,0:T(8,128)(2,1)} %x_ref.9) | copy-start | bytes 3145732
  32.8 0.9 copy-start.4
  33.7 0.7 copy-start.5
  46.7 5.7 %collective-permute-start.13 = (bf16[8,4096]{1,0:T(8,128)(2,1)S(1)}, bf16[8,4096]{1,0:T(8,128)(2,1)S(1)}, u32[]{:S(2)}, u32[]{:S(2)}) collective-permute-start(bf16[8,4096]{1,0:T(8,128)(2,1)S(1)} %get-tuple-element.32), channel_id=1, source_target_pairs={{0,4},{1,5},{2,6},{3,7},{4,8},{5,9},{6,10},{7,11},{8,12},{9,13},{1... | collective-permute-start | bytes 196616 | tf_op jit(solution)/shard_map/ppermute | solution.py:352
  46.7 8.3 %collective-permute-start.14 = (bf16[8,4096]{1,0:T(8,128)(2,1)S(1)}, bf16[8,4096]{1,0:T(8,128)(2,1)S(1)}, u32[]{:S(2)}, u32[]{:S(2)}) collective-permute-start(bf16[8,4096]{1,0:T(8,128)(2,1)S(1)} %get-tuple-element.33), channel_id=1, source_target_pairs={{0,8},{1,9},{2,10},{3,11},{4,12},{5,13},{6,14},{7,15},{8,0},{9,1},... | collective-permute-start | bytes 196616 | tf_op jit(solution)/shard_map/ppermute | solution.py:352
  46.8 8.7 %collective-permute-start.15 = (bf16[8,4096]{1,0:T(8,128)(2,1)S(1)}, bf16[8,4096]{1,0:T(8,128)(2,1)S(1)}, u32[]{:S(2)}, u32[]{:S(2)}) collective-permute-start(bf16[8,4096]{1,0:T(8,128)(2,1)S(1)} %get-tuple-element.34), channel_id=1, source_target_pairs={{0,12},{1,13},{2,14},{3,15},{4,0},{5,1},{6,2},{7,3},{8,4},{9,5},{1... | collective-permute-start | bytes 196616 | tf_op jit(solution)/shard_map/ppermute | solution.py:352
  48.8 6.8 %collective-permute-start.20 = (bf16[8,4096]{1,0:T(8,128)(2,1)S(1)}, bf16[8,4096]{1,0:T(8,128)(2,1)S(1)}, u32[]{:S(2)}, u32[]{:S(2)}) collective-permute-start(bf16[8,4096]{1,0:T(8,128)(2,1)S(1)} %get-tuple-element.28._.refs_0_), channel_id=1, source_target_pairs={{0,1},{1,0},{2,3},{3,2},{4,5},{5,4},{6,7},{7,6},{8,9},{9,8},{10,11... | collective-permute-start | bytes 196616 | tf_op jit(solution)/shard_map/ppermute | solution.py:352
  48.8 8.4 %collective-permute-start.16 = (bf16[8,4096]{1,0:T(8,128)(2,1)S(1)}, bf16[8,4096]{1,0:T(8,128)(2,1)S(1)}, u32[]{:S(2)}, u32[]{:S(2)}) collective-permute-start(bf16[8,4096]{1,0:T(8,128)(2,1)S(1)} %get-tuple-element.28._.refs_0_), channel_id=1, source_target_pairs={{0,2},{1,3},{2,0},{3,1},{4,6},{5,7},{6,4},{7,5},{8,10},{9,11},{10,... | collective-permute-start | bytes 196616 | tf_op jit(solution)/shard_map/ppermute | solution.py:352
  52.3 13.4 %collective-permute-start.21 = (bf16[8,4096]{1,0:T(8,128)(2,1)S(1)}, bf16[8,4096]{1,0:T(8,128)(2,1)S(1)}, u32[]{:S(2)}, u32[]{:S(2)}) collective-permute-start(bf16[8,4096]{1,0:T(8,128)(2,1)S(1)} %collective-permute-done.13.refs_1_), channel_id=1, source_target_pairs={{0,1},{1,0},{2,3},{3,2},{4,5},{5,4},{6,7},{7,6},{8,9},{9,8},{10,11... | collective-permute-start | bytes 196616 | tf_op jit(solution)/shard_map/ppermute | solution.py:352
  55.0 10.8 %collective-permute-start.17 = (bf16[8,4096]{1,0:T(8,128)(2,1)S(1)}, bf16[8,4096]{1,0:T(8,128)(2,1)S(1)}, u32[]{:S(2)}, u32[]{:S(2)}) collective-permute-start(bf16[8,4096]{1,0:T(8,128)(2,1)S(1)} %collective-permute-done.13.refs_1_), channel_id=1, source_target_pairs={{0,2},{1,3},{2,0},{3,1},{4,6},{5,7},{6,4},{7,5},{8,10},{9,11},{10,... | collective-permute-start | bytes 196616 | tf_op jit(solution)/shard_map/ppermute | solution.py:352
  55.5 10.8 %collective-permute-start.22 = (bf16[8,4096]{1,0:T(8,128)(2,1)S(1)}, bf16[8,4096]{1,0:T(8,128)(2,1)S(1)}, u32[]{:S(2)}, u32[]{:S(2)}) collective-permute-start(bf16[8,4096]{1,0:T(8,128)(2,1)S(1)} %collective-permute-done.14.refs_2_), channel_id=1, source_target_pairs={{0,1},{1,0},{2,3},{3,2},{4,5},{5,4},{6,7},{7,6},{8,9},{9,8},{10,11... | collective-permute-start | bytes 196616 | tf_op jit(solution)/shard_map/ppermute | solution.py:352
  55.5 10.9 %collective-permute-start.18 = (bf16[8,4096]{1,0:T(8,128)(2,1)S(1)}, bf16[8,4096]{1,0:T(8,128)(2,1)S(1)}, u32[]{:S(2)}, u32[]{:S(2)}) collective-permute-start(bf16[8,4096]{1,0:T(8,128)(2,1)S(1)} %collective-permute-done.14.refs_2_), channel_id=1, source_target_pairs={{0,2},{1,3},{2,0},{3,1},{4,6},{5,7},{6,4},{7,5},{8,10},{9,11},{10,... | collective-permute-start | bytes 196616 | tf_op jit(solution)/shard_map/ppermute | solution.py:352
  57.1 9.7 %collective-permute-start.19 = (bf16[8,4096]{1,0:T(8,128)(2,1)S(1)}, bf16[8,4096]{1,0:T(8,128)(2,1)S(1)}, u32[]{:S(2)}, u32[]{:S(2)}) collective-permute-start(bf16[8,4096]{1,0:T(8,128)(2,1)S(1)} %collective-permute-done.15.refs_3_), channel_id=1, source_target_pairs={{0,2},{1,3},{2,0},{3,1},{4,6},{5,7},{6,4},{7,5},{8,10},{9,11},{10,... | collective-permute-start | bytes 196616 | tf_op jit(solution)/shard_map/ppermute | solution.py:352
  65.7 9.5 %collective-permute-start.23 = (bf16[8,4096]{1,0:T(8,128)(2,1)S(1)}, bf16[8,4096]{1,0:T(8,128)(2,1)S(1)}, u32[]{:S(2)}, u32[]{:S(2)}) collective-permute-start(bf16[8,4096]{1,0:T(8,128)(2,1)S(1)} %collective-permute-done.15.refs_3_), channel_id=1, source_target_pairs={{0,1},{1,0},{2,3},{3,2},{4,5},{5,4},{6,7},{7,6},{8,9},{9,8},{10,11... | collective-permute-start | bytes 196616 | tf_op jit(solution)/shard_map/ppermute | solution.py:352
  65.8 9.4 %collective-permute-start.24 = (bf16[8,4096]{1,0:T(8,128)(2,1)S(1)}, bf16[8,4096]{1,0:T(8,128)(2,1)S(1)}, u32[]{:S(2)}, u32[]{:S(2)}) collective-permute-start(bf16[8,4096]{1,0:T(8,128)(2,1)S(1)} %collective-permute-done.16.refs_4_), channel_id=1, source_target_pairs={{0,1},{1,0},{2,3},{3,2},{4,5},{5,4},{6,7},{7,6},{8,9},{9,8},{10,11... | collective-permute-start | bytes 196616 | tf_op jit(solution)/shard_map/ppermute | solution.py:352
  66.3 8.9 %collective-permute-start.25 = (bf16[8,4096]{1,0:T(8,128)(2,1)S(1)}, bf16[8,4096]{1,0:T(8,128)(2,1)S(1)}, u32[]{:S(2)}, u32[]{:S(2)}) collective-permute-start(bf16[8,4096]{1,0:T(8,128)(2,1)S(1)} %collective-permute-done.17.refs_5_), channel_id=1, source_target_pairs={{0,1},{1,0},{2,3},{3,2},{4,5},{5,4},{6,7},{7,6},{8,9},{9,8},{10,11... | collective-permute-start | bytes 196616 | tf_op jit(solution)/shard_map/ppermute | solution.py:352
  66.4 8.8 %collective-permute-start.26 = (bf16[8,4096]{1,0:T(8,128)(2,1)S(1)}, bf16[8,4096]{1,0:T(8,128)(2,1)S(1)}, u32[]{:S(2)}, u32[]{:S(2)}) collective-permute-start(bf16[8,4096]{1,0:T(8,128)(2,1)S(1)} %collective-permute-done.18.refs_6_), channel_id=1, source_target_pairs={{0,1},{1,0},{2,3},{3,2},{4,5},{5,4},{6,7},{7,6},{8,9},{9,8},{10,11... | collective-permute-start | bytes 196616 | tf_op jit(solution)/shard_map/ppermute | solution.py:352
  66.8 8.4 %collective-permute-start.27 = (bf16[8,4096]{1,0:T(8,128)(2,1)S(1)}, bf16[8,4096]{1,0:T(8,128)(2,1)S(1)}, u32[]{:S(2)}, u32[]{:S(2)}) collective-permute-start(bf16[8,4096]{1,0:T(8,128)(2,1)S(1)} %collective-permute-done.19.refs_7_), channel_id=1, source_target_pairs={{0,1},{1,0},{2,3},{3,2},{4,5},{5,4},{6,7},{7,6},{8,9},{9,8},{10,11... | collective-permute-start | bytes 196616 | tf_op jit(solution)/shard_map/ppermute | solution.py:352
  77.2 2.0 %collective-permute-start.28 = (bf16[64,4096]{1,0:T(8,128)(2,1)S(1)}, bf16[64,4096]{1,0:T(8,128)(2,1)S(1)}, u32[]{:S(2)}, u32[]{:S(2)}) collective-permute-start(bf16[64,4096]{1,0:T(8,128)(2,1)S(1)} %get-tuple-element.42), channel_id=1, source_target_pairs={{0,1},{1,0},{2,3},{3,2},{4,5},{5,4},{6,7},{7,6},{8,9},{9,8},{10,11... | collective-permute-start | bytes 1572872 | tf_op jit(solution)/shard_map/ppermute | solution.py:352
  79.4 8.7 %collective-permute-start.29 = (bf16[32,4096]{1,0:T(8,128)(2,1)S(1)}, bf16[32,4096]{1,0:T(8,128)(2,1)S(1)}, u32[]{:S(2)}, u32[]{:S(2)}) collective-permute-start(bf16[32,4096]{1,0:T(8,128)(2,1)S(1)} %slice.35), channel_id=1, source_target_pairs={{0,2},{1,3},{2,0},{3,1},{4,6},{5,7},{6,4},{7,5},{8,10},{9,11},{10,... | collective-permute-start | bytes 786440 | tf_op jit(solution)/shard_map/ppermute | solution.py:352
  88.1 10.2 %collective-permute-start.32 = (bf16[8,4096]{1,0:T(8,128)(2,1)S(1)}, bf16[8,4096]{1,0:T(8,128)(2,1)S(1)}, u32[]{:S(2)}, u32[]{:S(2)}) collective-permute-start(bf16[8,4096]{1,0:T(8,128)(2,1)S(1)} %get-tuple-element.43), channel_id=1, source_target_pairs={{0,4},{1,5},{2,6},{3,7},{4,8},{5,9},{6,10},{7,11},{8,12},{9,13},{1... | collective-permute-start | bytes 196616 | tf_op jit(solution)/shard_map/ppermute | solution.py:352
  88.1 10.2 %collective-permute-start.31 = (bf16[8,4096]{1,0:T(8,128)(2,1)S(1)}, bf16[8,4096]{1,0:T(8,128)(2,1)S(1)}, u32[]{:S(2)}, u32[]{:S(2)}) collective-permute-start(bf16[8,4096]{1,0:T(8,128)(2,1)S(1)} %get-tuple-element.44), channel_id=1, source_target_pairs={{0,8},{1,9},{2,10},{3,11},{4,12},{5,13},{6,14},{7,15},{8,0},{9,1},... | collective-permute-start | bytes 196616 | tf_op jit(solution)/shard_map/ppermute | solution.py:352
  88.2 10.1 %copy-start.7 = (s32[128,4]{0,1:T(4,128)S(1)}, s32[128,4]{0,1:T(4,128)}, u32[]{:S(2)}) copy-start(s32[128,4]{0,1:T(4,128)} %param.17) | copy-start | bytes 6148
  88.2 10.1 %copy-start.9 = (f32[128,4]{0,1:T(4,128)S(1)}, f32[128,4]{0,1:T(4,128)}, u32[]{:S(2)}) copy-start(f32[128,4]{0,1:T(4,128)} %param.18) | copy-start | bytes 6148
  88.3 10.1 %collective-permute-start.30 = (bf16[8,4096]{1,0:T(8,128)(2,1)S(1)}, bf16[8,4096]{1,0:T(8,128)(2,1)S(1)}, u32[]{:S(2)}, u32[]{:S(2)}) collective-permute-start(bf16[8,4096]{1,0:T(8,128)(2,1)S(1)} %get-tuple-element.45), channel_id=1, source_target_pairs={{0,12},{1,13},{2,14},{3,15},{4,0},{5,1},{6,2},{7,3},{8,4},{9,5},{1... | collective-permute-start | bytes 196616 | tf_op jit(solution)/shard_map/ppermute | solution.py:352
